TPU v7x, 512 devices: a whole 4x4x16 slice. The times are simulated.
512 devices in a mesh: row: 16 (over x, z_hi, core), col: 32 (over z_lo, y).
Axes of the slice: x: 4, y: 4, z: 16 (z_hi: 2, z_lo: 8; z = z_hi * 8 + z_lo), core: 2. Of those that a mesh axis runs over, the one named last changes fastest.
Arguments:
- pair_state: bfloat16 [384, 384, 128], P('row', 'col'), may hold values from -6 to 6
- outgoing_input: bfloat16 [128, 640], replicated, may hold values from -0.5 to 0.5
- outgoing_output: bfloat16 [128, 128], replicated, may hold values from -0.5 to 0.5
- incoming_input: bfloat16 [128, 640], replicated, may hold values from -0.5 to 0.5
- incoming_output: bfloat16 [128, 128], replicated, may hold values from -0.5 to 0.5
- transition_input: bfloat16 [128, 1024], replicated, may hold values from -0.5 to 0.5
- transition_output: bfloat16 [512, 128], replicated, may hold values from -0.25 to 0.25
Outputs:
- pair_result: bfloat16 [384, 384, 128], P('row', 'col')
All inputs are finite; a program needn't handle non-finite values.
Results may differ from a plain program's by a relative error of at most 0.02.
Values may be sent and summed in bfloat16 or wider, within the bound.
A program may use at most 64 MiB of HBM per device.

v0:
```python
import jax
import jax.numpy as jnp
from jax import lax
from jax.sharding import PartitionSpec as P

norm_eps = 1e-05


def broadcast(block, axis, owner):
    block = jnp.where(lax.axis_index(axis) == owner, block, jnp.zeros_like(block))
    return lax.psum(block, axis)


def layer_norm(values):
    centred = values - jnp.mean(values, axis=-1, keepdims=True)
    spread = jnp.mean(centred * centred, axis=-1, keepdims=True)
    return centred * lax.rsqrt(spread + norm_eps)


def projections(state_tile, weight):
    channels = state_tile.shape[-1]
    normed = layer_norm(state_tile.astype(jnp.float32)).astype(jnp.bfloat16)
    projected = jnp.dot(normed, weight, preferred_element_type=jnp.float32)
    left_edge = (
        jax.nn.sigmoid(projected[..., :channels]) * projected[..., channels : 2 * channels]
    ).astype(jnp.bfloat16)
    right_edge = (
        jax.nn.sigmoid(projected[..., 2 * channels : 3 * channels])
        * projected[..., 3 * channels : 4 * channels]
    ).astype(jnp.bfloat16)
    out_gate = jax.nn.sigmoid(projected[..., 4 * channels :])
    return (left_edge, right_edge, out_gate)


def finish_update(state_tile, combined, out_gate, weight):
    normed = layer_norm(combined).astype(jnp.bfloat16)
    update = jnp.dot(normed, weight, preferred_element_type=jnp.float32)
    return (state_tile.astype(jnp.float32) + out_gate * update).astype(jnp.bfloat16)


def body(
    pair_state,
    outgoing_input,
    outgoing_output,
    incoming_input,
    incoming_output,
    transition_input,
    transition_output,
):
    rows_count = lax.axis_size("row")
    cols_count = lax.axis_size("col")
    tile_rows, tile_cols, channels = pair_state.shape
    blocks_per_row = cols_count // rows_count
    row_index = lax.axis_index("row")
    col_index = lax.axis_index("col")
    left_edge, right_edge, out_gate = projections(pair_state, outgoing_input)
    full_rows = lax.all_gather(right_edge, "col", axis=1, tiled=True)
    needed = lax.dynamic_slice_in_dim(
        full_rows, col_index % blocks_per_row * tile_cols, tile_cols, 0
    )
    right_rows = broadcast(needed, "row", col_index // blocks_per_row)
    matching = right_rows
    combined = jnp.einsum(
        "ikc,jkc->ijc",
        lax.all_gather(left_edge, "col", axis=1, tiled=True),
        matching,
        preferred_element_type=jnp.float32,
    )
    after_out = finish_update(pair_state, combined, out_gate, outgoing_output)
    left_edge, right_edge, out_gate = projections(after_out, incoming_input)
    columns = lax.all_gather(left_edge, "row", axis=0, tiled=True)
    gathered = []
    for offset in range(blocks_per_row):
        gathered.append(broadcast(columns, "col", row_index * blocks_per_row + offset))
    left_cols = jnp.concatenate(gathered, axis=1)
    matching = left_cols
    combined = jnp.einsum(
        "kic,kjc->ijc",
        matching,
        lax.all_gather(right_edge, "row", axis=0, tiled=True),
        preferred_element_type=jnp.float32,
    )
    after_in = finish_update(after_out, combined, out_gate, incoming_output)
    hidden_units = transition_output.shape[0]
    normed = layer_norm(after_in.astype(jnp.float32)).astype(jnp.bfloat16)
    hidden = jnp.dot(normed, transition_input, preferred_element_type=jnp.float32)
    mixed = (jax.nn.silu(hidden[..., :hidden_units]) * hidden[..., hidden_units:]).astype(
        jnp.bfloat16
    )
    result = after_in.astype(jnp.float32) + jnp.dot(
        mixed, transition_output, preferred_element_type=jnp.float32
    )
    return result.astype(jnp.bfloat16)


def solution(mesh):
    placed = (P("row", "col", None), P(), P(), P(), P(), P(), P())
    return jax.shard_map(
        body, mesh=mesh, in_specs=placed, out_specs=P("row", "col", None), check_vma=False
    )
```

profile of v0, /device:TPU:1, one launch (start us, length us, event | category | flops | bytes accessed | tf_op | source)
XLA Modules:
  0.0 1401.1 jit_solution(10317280791922409444)
XLA Ops:
  6.5 1.0 convert_reduce_fusion
  7.6 1.1 fusion.17
  8.7 1.3 fusion.15
  10.0 0.9 copy-done.1
  10.9 0.7 fusion.30
  11.7 0.7 all-gather.7.cloned.1.call-update
  12.5 208.6 %all-gather.5.cloned.1.call-done = bf16[24,384,128]{2,0,1:T(8,128)(2,1)} async-done(((bf16[24,12,128]{2,0,1:T(8,128)(2,1)}), bf16[24,384,128]{2,0,1:T(8,128)(2,1)}) %all-gather.5.cloned.1.call-update) | async-done | bytes 2359312 | tf_op jit(solution)/shard_map/all_gather | solution.py:57
  221.1 2.4 constant_dynamic-slice_fusion
  223.5 1.6 copy.26
  225.2 1.3 broadcast_select_fusion
  226.6 219.6 %all-gather.7.cloned.1.call-done = bf16[24,384,128]{2,0,1:T(8,128)(2,1)} async-done(((bf16[24,12,128]{2,0,1:T(8,128)(2,1)}), bf16[24,384,128]{2,0,1:T(8,128)(2,1)}) %all-gather.7.cloned.1.call-update) | async-done | bytes 2359312 | tf_op jit(solution)/shard_map/all_gather | solution.py:65
  446.2 10.9 copy.21
  457.1 331.5 %all-reduce.4.cloned.1.call-done = bf16[12,384,128]{1,0,2:T(8,128)(2,1)} async-done(((bf16[12,384,128]{1,0,2:T(8,128)(2,1)}), bf16[12,384,128]{1,0,2:T(8,128)(2,1)}) %all-reduce.4.cloned.1.call-update) | async-done | bytes 1179664 | tf_op jit(solution)/shard_map/psum | solution.py:11
  788.6 7.3 fusion.58
  796.0 0.3 copy.22
  796.7 1.3 fusion.56
  798.2 0.4 fusion.13
  798.5 0.7 fusion.19
  799.4 0.5 all-gather.9.cloned.1.call-update
  800.0 78.6 %all-gather.11.cloned.1.call-done = bf16[384,12,128]{2,0,1:T(8,128)(2,1)} async-done(((bf16[24,12,128]{2,0,1:T(8,128)(2,1)}), bf16[384,12,128]{2,0,1:T(8,128)(2,1)}) %all-gather.11.cloned.1.call-update) | async-done | bytes 1179664 | tf_op jit(solution)/shard_map/all_gather | solution.py:71
  878.5 2.9 broadcast_select_fusion.2
  881.5 69.9 %all-gather.9.cloned.1.call-done = bf16[384,12,128]{2,0,1:T(8,128)(2,1)} async-done(((bf16[24,12,128]{2,0,1:T(8,128)(2,1)}), bf16[384,12,128]{2,0,1:T(8,128)(2,1)}) %all-gather.9.cloned.1.call-update) | async-done | bytes 1179664 | tf_op jit(solution)/shard_map/all_gather | solution.py:80
  951.4 2.9 copy.23
  954.4 429.3 %all-reduce.6.cloned.1.call-done = (bf16[384,12,128]{2,0,1:T(8,128)(2,1)}, bf16[384,12,128]{2,0,1:T(8,128)(2,1)}) async-done(((bf16[384,12,128]{2,0,1:T(8,128)(2,1)}, bf16[384,12,128]{2,0,1:T(8,128)(2,1)}), (bf16[384,12,128]{2,0,1:T(8,128)(2,1)}, bf16[384,12,128]{2,0,1:T(8,128)(2,1)})) %all-reduce.6.cloned.1.call-update) | async-done | bytes 2359312 | tf_op jit(solution)/shard_map/psum | solution.py:11
  1383.7 1.8 pad_maximum_fusion
  1385.5 2.9 copy.24
  1388.4 3.2 fusion.59
  1391.6 0.3 copy.25
  1392.3 0.4 fusion.57
  1392.6 0.2 multiply_reduce_fusion
  1392.9 0.4 fusion.9
  1393.2 1.0 fusion.4
  (38 shorter events, 1.1 us)
Async XLA Ops:
  6.5 1386.3 %copy-start = (bf16[128,1024]{1,0:T(8,128)(2,1)S(1)}, bf16[128,1024]{1,0:T(8,128)(2,1)}, u32[]{:S(2)}) copy-start(bf16[128,1024]{1,0:T(8,128)(2,1)} %param.12) | copy-start | bytes 786436
  6.5 214.6 %all-gather.5.cloned.1.call-start = ((), (), s32[]{:S(2)}) async-start(), calls=%async_computation | async-start | bytes 2433024 | tf_op jit(solution)/shard_map/all_gather | solution.py:57
  10.0 0.9 copy-start.1
  11.7 434.5 %all-gather.7.cloned.1.call-start = ((), (), s32[]{:S(2)}) async-start(), calls=%async_computation.2 | async-start | bytes 2433024 | tf_op jit(solution)/shard_map/all_gather | solution.py:65
  12.4 776.2 %all-reduce.4.cloned.1.call-start = ((), (), s32[]{:S(2)}) async-start(), calls=%async_computation.1 | async-start | bytes 3145728 | tf_op jit(solution)/shard_map/psum | solution.py:11
  226.5 652.0 %all-gather.11.cloned.1.call-start = ((), (), s32[]{:S(2)}) async-start(), calls=%async_computation.4 | async-start | bytes 1253376 | tf_op jit(solution)/shard_map/all_gather | solution.py:71
  457.1 339.6 %copy-start.2 = (bf16[24,12,128]{2,0,1:T(8,128)(2,1)S(1)}, bf16[24,12,128]{2,0,1:T(8,128)(2,1)}, u32[]{:S(2)}) copy-start(bf16[24,12,128]{2,0,1:T(8,128)(2,1)} %param.7) | copy-start | bytes 221188
  457.1 339.6 %copy-start.5 = (bf16[128,128]{1,0:T(8,128)(2,1)S(1)}, bf16[128,128]{1,0:T(8,128)(2,1)}, u32[]{:S(2)}) copy-start(bf16[128,128]{1,0:T(8,128)(2,1)} %param.9) | copy-start | bytes 98308
  796.0 2.2 copy-start.3
  799.3 152.1 %all-gather.9.cloned.1.call-start = ((), (), s32[]{:S(2)}) async-start(), calls=%async_computation.3 | async-start | bytes 1253376 | tf_op jit(solution)/shard_map/all_gather | solution.py:80
  799.9 583.8 %all-reduce.6.cloned.1.call-start = ((), (), s32[]{:S(2)}) async-start(), calls=%async_computation.5 | async-start | bytes 4718592 | tf_op jit(solution)/shard_map/psum | solution.py:11
  1388.4 3.9 copy-start.6
  1391.9 1.3 copy-start.4
Sparse Core Ops, SparseCore 0:
  11.8 209.2 all-gather.4
  223.2 222.9 all-gather.6
  449.1 339.4 all-reduce.3
  799.4 79.0 all-gather.10
  882.0 69.3 all-gather.8
  954.5 429.1 all-reduce.5
where the time goes:
time: 1420 us; the launch traced here: 1400 us
  waiting for transfers between devices  1340 us (94%)
  local copies, waits for them, and re-layouts  22.4 us (2%)
  matrix products  15.1 us (1%)
    psum x2, waiting for transfers between devices, broadcast(): return lax.psum(block, axis)  761 us
    all_gather x1, waiting for transfers between devices, body(): lax.all_gather(left_edge, 'col', axis=1, tiled=True)  220 us
    all_gather x1, waiting for transfers between devices, body(): full_rows = lax.all_gather(right_edge, 'col', axis=1, tiled=True)  209 us
    all_gather x1, waiting for transfers between devices, body(): columns = lax.all_gather(left_edge, 'row', axis=0, tiled=True)  78.6 us
    all_gather x1, waiting for transfers between devices, body(): lax.all_gather(right_edge, 'row', axis=0, tiled=True)  69.9 us
  transfers between devices with their start and end apart: 6, of which 6 were waited for; matrix products, arithmetic and copies ran while one was open for 2% of the time, Pallas kernels for 0%

commit v1 on v0

v1 whole, which is shorter than its diff:
```python
import jax
import jax.numpy as jnp
from jax import lax
from jax.experimental import pallas as pl
from jax.experimental.pallas import tpu as pltpu
from jax.sharding import PartitionSpec as P

MESH = pl.DeviceIdType.MESH
norm_eps = 1e-05
f32 = jnp.float32
bf16 = jnp.bfloat16


def roll_lanes(values, shift):
    return pltpu.roll(values, shift, 1)


def swap_lanes(parts, width, roll):
    lane = lax.broadcasted_iota(jnp.int32, parts[0].shape, 1)
    parts = list(parts)
    for bit in (1, 2, 4):
        low = (lane & (bit * width)) == 0
        for a in range(8):
            if a & bit == 0:
                first, second = parts[a], parts[a | bit]
                parts[a] = jnp.where(low, first, roll(second, bit * width))
                parts[a | bit] = jnp.where(low, roll(first, 128 - bit * width), second)
    return parts


def layer_norm(values):
    centred = values - jnp.mean(values, axis=-1, keepdims=True)
    spread = jnp.mean(centred * centred, axis=-1, keepdims=True)
    return centred * lax.rsqrt(spread + norm_eps)


def nt(a, b):
    return lax.dot_general(a, b, (((1,), (1,)), ((), ())), preferred_element_type=f32)


def nn(a, b):
    return jnp.dot(a, b, preferred_element_type=f32)


def widen(rows, columns):
    row = lax.broadcasted_iota(jnp.int32, (rows, columns), 0)
    column = lax.broadcasted_iota(jnp.int32, (rows, columns), 1)
    inside = column & 15
    hit = (row == (column >> 4) * 12 + inside) & (inside < 12)
    return jnp.where(hit, 1.0, 0.0).astype(bf16)


def channel_order():
    row = lax.broadcasted_iota(jnp.int32, (128, 128), 0)
    column = lax.broadcasted_iota(jnp.int32, (128, 128), 1)
    return jnp.where(column == (row & 7) * 16 + (row >> 3), 1.0, 0.0).astype(bf16)


def edges(normed, w_t):
    ordered = jnp.concatenate(
        [normed[(il * 3 + ih) * 16 : (il * 3 + ih + 1) * 16] for ih in range(3) for il in range(8)], axis=0
    )
    projected = nt(w_t, ordered)
    left = jax.nn.sigmoid(projected[0:128]) * projected[128:256]
    right = jax.nn.sigmoid(projected[256:384]) * projected[384:512]
    return left.astype(bf16), right.astype(bf16)


def regroup(blocks, roll):
    for core in range(2):
        for ih in range(3):
            parts = swap_lanes([blocks(core, s, y, ih) for s in range(2) for y in range(4)], 16, roll)
            for il in range(8):
                yield core * 24 + ih * 8 + il, parts[il]


def split_pair(first, second, roll):
    low = lax.broadcasted_iota(jnp.int32, first.shape, 1) < 64
    return jnp.where(low, first, roll(second, 64)), jnp.where(low, roll(first, 64), second)


def product_out(left, right):
    total = nt(left, right).astype(bf16)
    return nn(total, widen(384, 512))


def product_in(left, right):
    turned = nt(widen(96, 128), left).astype(bf16)
    return nn(turned, right)


def parcels(total, roll):
    for zh in range(2):
        for t in range(4):
            tile = total[zh * 48 : (zh + 1) * 48, t * 128 : (t + 1) * 128]
            even, odd = split_pair(tile[0:24], tile[24:48], roll)
            yield zh * 8 + 2 * t, even
            yield zh * 8 + 2 * t + 1, odd


def finish(state, combined, gate, weight):
    update = nn(layer_norm(combined).astype(bf16), weight)
    return (state.astype(f32) + gate * update).astype(bf16)


def kernel(
    x_ref, w1_ref, o1_ref, w2_ref, o2_ref, t1_ref, t2_ref, out_ref,
    a1s, a1r, a2f, a2s, a2r, l2, l2s, bl, br, c1s, c1r, c2s, c2r,
    a1_send, a1_recv, a2_send, a2_recv, b_send, b_recv, bl_send, bl_recv, c1_send, c1_recv, c2_send, c2_recv,
):
    row, col = lax.axis_index("row"), lax.axis_index("col")
    x, zh, core = row // 4, (row // 2) % 2, row % 2
    zl, y = col // 4, col % 4
    z, p = zh * 8 + zl, y * 2 + core

    def at_p(other):
        return ((x * 2 + zh) * 2 + other % 2, zl * 4 + other // 2)

    def at_z(other):
        return ((x * 2 + other // 8) * 2 + core, (other % 8) * 4 + y)

    def at_x(other):
        return ((other * 2 + zh) * 2 + core, col)

    barrier = pltpu.get_barrier_semaphore()
    for me, count, place in ((p, 8, at_p), (z, 16, at_z), (x, 4, at_x)):
        for step in range(1, count):
            pl.semaphore_signal(
                barrier, inc=1, device_id=place(lax.rem(me + step, count)), device_id_type=MESH
            )

    sent = []

    def exchange(source, target, me, count, place, send, recv):
        for step in range(1, count):
            other = lax.rem(me + step, count)
            copy = pltpu.make_async_remote_copy(
                src_ref=source(other), dst_ref=target.at[me], send_sem=send.at[step], recv_sem=recv.at[me],
                device_id=place(other), device_id_type=MESH,
            )
            copy.start()
            sent.append(copy)

    def arrive(source, target, me, count, place, send, recv):
        for step in range(1, count):
            other = lax.rem(me + step, count)
            pltpu.make_async_remote_copy(
                src_ref=source(other), dst_ref=target.at[other], send_sem=send.at[step], recv_sem=recv.at[other],
                device_id=place(other), device_id_type=MESH,
            ).wait_recv()

    def triangle(n, state, w_ref, o_ref):
        normed = layer_norm(state.astype(f32)).astype(bf16)
        left, right = edges(normed, w_ref[:, 0:512].T)
        for other in range(8):
            for s, edge in enumerate((left, right)):
                for ih in range(3):
                    a1s[n, other, s, ih] = edge[other * 16 : other * 16 + 16, ih * 128 : ih * 128 + 128]
        if n == 0:
            pl.semaphore_wait(barrier, 25)
        a1 = (lambda other: a1s.at[n, other], a1r.at[n], p, 8, at_p, a1_send.at[n], a1_recv.at[n])
        exchange(*a1)
        a1r[n, p] = a1s[n, p]
        gate = jax.nn.sigmoid(nn(normed, w_ref[:, 512:640]))
        weight = nn(channel_order(), o_ref[...]).astype(bf16)
        arrive(*a1)

        for i, rows in regroup(lambda core, s, y, ih: a1r[n, y * 2 + core, s, ih].astype(f32), roll_lanes):
            a2f[pl.ds(i, 16, stride=48), :] = rows
        for c in range(16):
            a2s[n, c] = a2f[c * 48 : c * 48 + 48, :].astype(bf16)
        a2 = (lambda other: a2s.at[n, other], a2r.at[n], z, 16, at_z, a2_send.at[n], a2_recv.at[n])
        exchange(*a2)
        a2r[n, z] = a2s[n, z]
        arrive(*a2)

        for half in range(2):
            for t in range(4):
                first, second = split_pair(
                    a2r[n, half * 8 + 2 * t].astype(f32), a2r[n, half * 8 + 2 * t + 1].astype(f32), roll_lanes
                )
                l2s[n, t, half * 48 : half * 48 + 48, :] = first.astype(bf16)
                l2[n, half * 48 : half * 48 + 48, t * 128 : t * 128 + 128] = second.astype(bf16)
        b = (lambda other: l2.at[n], br.at[n], x, 4, at_x, b_send.at[n], b_recv.at[n])
        exchange(*b)
        if n == 1:
            bl_args = (lambda other: l2s.at[n, other], bl, x, 4, at_x, bl_send, bl_recv)
            exchange(*bl_args)
            bl[x] = l2s[n, x]
        br[n, x] = l2[n]
        arrive(*b)
        rights = jnp.concatenate([br[n, other] for other in range(4)], axis=0)
        if n == 0:
            lefts = jnp.concatenate([l2s[n, t] for t in range(4)], axis=1)
            total = product_out(lefts, rights)
        else:
            arrive(*bl_args)
            total = product_in(jnp.concatenate([bl[other] for other in range(4)], axis=0), rights)

        for other, rows in parcels(total, roll_lanes):
            c1s[n, other] = rows.astype(bf16)
        c1 = (lambda other: c1s.at[n, other], c1r.at[n], z, 16, at_z, c1_send.at[n], c1_recv.at[n])
        exchange(*c1)
        c1r[n, z] = c1s[n, z]
        arrive(*c1)
        received = [c1r[n, c].astype(f32) for c in range(16)]
        for ih in range(3):
            turned = jnp.concatenate([part[ih * 8 : ih * 8 + 8] for part in received], axis=0).T
            for there in range(2):
                for far in range(4):
                    start = (there * 4 + far) * 16
                    c2s[n, far * 2 + there, ih] = turned[start : start + 16].astype(bf16)
        c2 = (lambda other: c2s.at[n, other], c2r.at[n], p, 8, at_p, c2_send.at[n], c2_recv.at[n])
        exchange(*c2)
        c2r[n, p] = c2s[n, p]
        arrive(*c2)
        parts = swap_lanes([c2r[n, s].reshape(48, 128).astype(f32) for s in range(8)], 1, roll_lanes)
        return finish(state, jnp.concatenate(parts, axis=0), gate, weight)

    state = x_ref[...].reshape(384, 128)
    state = triangle(0, state, w1_ref, o1_ref)
    state = triangle(1, state, w2_ref, o2_ref)
    normed = layer_norm(state.astype(f32)).astype(bf16)
    hidden = nn(normed, t1_ref[...])
    mixed = (jax.nn.silu(hidden[:, :512]) * hidden[:, 512:]).astype(bf16)
    result = (state.astype(f32) + nn(mixed, t2_ref[...])).astype(bf16)
    out_ref[...] = result.reshape(8, 3, 16, 128)
    for copy in sent:
        copy.wait_send()


def body(pair_state, *weights):
    x = jnp.pad(pair_state, ((0, 0), (0, 4), (0, 0))).reshape(3, 8, 16, 128).transpose(1, 0, 2, 3)
    dma = pltpu.SemaphoreType.DMA
    out = pl.pallas_call(
        kernel,
        out_shape=jax.ShapeDtypeStruct((8, 3, 16, 128), bf16),
        in_specs=[pl.BlockSpec(memory_space=pltpu.VMEM)] * 7,
        out_specs=pl.BlockSpec(memory_space=pltpu.VMEM),
        scratch_shapes=[
            pltpu.VMEM((2, 8, 2, 3, 16, 128), bf16),
            pltpu.VMEM((2, 8, 2, 3, 16, 128), bf16),
            pltpu.VMEM((768, 128), f32),
            pltpu.VMEM((2, 16, 48, 128), bf16),
            pltpu.VMEM((2, 16, 48, 128), bf16),
            pltpu.VMEM((2, 96, 512), bf16),
            pltpu.VMEM((2, 4, 96, 128), bf16),
            pltpu.VMEM((4, 96, 128), bf16),
            pltpu.VMEM((2, 4, 96, 512), bf16),
            pltpu.VMEM((2, 16, 24, 128), bf16),
            pltpu.VMEM((2, 16, 24, 128), bf16),
            pltpu.VMEM((2, 8, 3, 16, 128), bf16),
            pltpu.VMEM((2, 8, 3, 16, 128), bf16),
            dma((2, 8)), dma((2, 8)),
            dma((2, 16)), dma((2, 16)),
            dma((2, 4)), dma((2, 4)),
            dma((4,)), dma((4,)),
            dma((2, 16)), dma((2, 16)),
            dma((2, 8)), dma((2, 8)),
        ],
        compiler_params=pltpu.CompilerParams(
            collective_id=0, has_side_effects=True, vmem_limit_bytes=48 * 2**20
        ),
    )(x, *weights)
    return out.transpose(1, 0, 2, 3).reshape(24, 16, 128)[:, :12]


def solution(mesh):
    placed = (P("row", "col", None), P(), P(), P(), P(), P(), P())
    return jax.shard_map(
        body, mesh=mesh, in_specs=placed, out_specs=P("row", "col", None), check_vma=False
    )
```

time: 1420 us -> 101 us (0.07); the launches traced: 1400 us -> 100 us
  waiting for transfers between devices: 1340 us -> 0 us
  Pallas kernels: 0 us -> 95.4 us
  local copies, waits for them, and re-layouts: 22.4 us -> 4.99 us
  matrix products: 15.1 us -> 0 us
    psum x2 -> x0, waiting for transfers between devices: 761 us -> none  [broadcast(): return lax.psum(block, axis)]
    all_gather x4 -> x0, waiting for transfers between devices: 577 us -> none  [the longest x1 220 us: body(): lax.all_gather(left_edge, 'col', axis=1, tiled=True)]
    pallas_call x0 -> x1, Pallas kernels: none -> 95.4 us  [body(): pl.pallas_call(kernel, out_shape=jax.ShapeDtypeStruct((8, 3, 16, 128), bf...]
    dot_general x8 -> x0, matrix products: 15.1 us -> none  [the longest x1 7.35 us: body(): jnp.einsum('ikc,jkc->ijc', lax.all_gather(left_edge, 'col', axis=1, tiled...]
  transfers between devices with their start and end apart: 6 -> 0, of which waited for: 6 -> 0; matrix products, arithmetic and copies ran while one was open for 2% -> 0% of each run, Pallas kernels for 0% -> 0%
where the time goes in v1:
time: 101 us; the launch traced here: 100 us
  Pallas kernels  95.4 us (94%)
  local copies, waits for them, and re-layouts  4.99 us (5%)
    pallas_call x1, Pallas kernels, body(): pl.pallas_call(kernel, out_shape=jax.ShapeDtypeStruct((8, 3, 16, 128), bf...  95.4 us
    unnamed x13, local copies, waits for them, and re-layouts  4.3 us

profile of v1, /device:TPU:1, one launch (start us, length us, event | category | flops | bytes accessed | tf_op | source)
XLA Modules:
  0.0 100.4 jit_solution(46074449699154639)
XLA Ops:
  0.0 0.0 copy-start
  0.0 0.9 copy.8
  1.0 0.0 copy-start.1
  1.0 0.0 copy-start.3
  1.0 0.0 copy-done
  1.0 0.8 copy-done.1
  1.9 0.1 copy-done.3
  1.9 0.0 copy-start.2
  1.9 0.9 copy-done.2
  2.9 0.0 copy-start.4
  2.9 0.8 copy-done.4
  3.6 0.0 copy-start.5
  3.6 0.8 copy-done.5
  4.4 95.4 %shard_map.73 = bf16[8,3,16,128]{3,2,1,0:T(8,128)(2,1)S(1)} custom-call(bf16[8,3,16,128]{3,2,1,0:T(8,128)(2,1)S(1)} %bitcast.7, bf16[128,640]{1,0:T(8,128)(2,1)S(1)} %copy-done.1, bf16[128,128]{1,0:T(8,128)(2,1)S(1)} %copy-done.4, bf16[128,640]{1,0:T(8,128)(2,1)S(1)} %copy-done.2, bf16[128,128]{1,0:T(8,128)(2,1)S(1)} %copy-done.5, ...), custom_call_target="tpu_custom_call" | custom-call | tf_op jit(solution)/shard_map/pallas_call | solution.py:235
  99.8 0.7 copy.11
  (3 shorter events, 0.0 us)
Async XLA Ops:
  0.0 1.0 %copy-start = (bf16[128,1024]{1,0:T(8,128)(2,1)S(1)}, bf16[128,1024]{1,0:T(8,128)(2,1)}, u32[]{:S(2)}) copy-start(bf16[128,1024]{1,0:T(8,128)(2,1)} %t1_ref.1) | copy-start | bytes 786436
  1.0 0.9 copy-start.1
  1.0 1.0 copy-start.3
  1.9 0.9 copy-start.2
  2.9 0.8 copy-start.4
  3.6 0.8 copy-start.5

commit v2 on v1

v2 whole, which is shorter than its diff:
```python
import jax
import jax.numpy as jnp
from jax import lax
from jax.experimental import pallas as pl
from jax.experimental.pallas import tpu as pltpu
from jax.sharding import PartitionSpec as P

MESH = pl.DeviceIdType.MESH
norm_eps = 1e-05
f32 = jnp.float32
bf16 = jnp.bfloat16

Z_STEPS = (8, 7, 9, 6, 10, 5, 11, 4, 12, 3, 13, 2, 14, 1, 15)
RING = (2, 1, 3, 0)
P_STEPS = tuple((0, dy, dc) for dy in RING for dc in (1, 0) if (dy, dc) != (0, 0))
G_STEPS = tuple(
    sorted(
        ((dx, dy, dc) for dx in RING for dy in RING for dc in (1, 0) if (dx, dy, dc) != (0, 0, 0)),
        key=lambda step: -(min(step[0], 4 - step[0]) + min(step[1], 4 - step[1])),
    )
)


def roll_lanes(values, shift):
    return pltpu.roll(values, shift, 1)


def swap_lanes(parts, width, roll, bits=(1, 2, 4)):
    lane = lax.broadcasted_iota(jnp.int32, parts[0].shape, 1)
    parts = list(parts)
    for bit in bits:
        low = (lane & (bit * width)) == 0
        for a in range(len(parts)):
            if a & bit == 0:
                first, second = parts[a], parts[a | bit]
                parts[a] = jnp.where(low, first, roll(second, bit * width))
                parts[a | bit] = jnp.where(low, roll(first, 128 - bit * width), second)
    return parts


def layer_norm(values):
    centred = values - jnp.mean(values, axis=-1, keepdims=True)
    spread = jnp.mean(centred * centred, axis=-1, keepdims=True)
    return centred * lax.rsqrt(spread + norm_eps)


def nt(a, b):
    return lax.dot_general(a, b, (((1,), (1,)), ((), ())), preferred_element_type=f32)


def nn(a, b):
    return jnp.dot(a, b, preferred_element_type=f32)


def ones_where(shape, row_of):
    row = lax.broadcasted_iota(jnp.int32, shape, 0)
    column = lax.broadcasted_iota(jnp.int32, shape, 1)
    return jnp.where((row == row_of(column)) & ((column & 15) < 12), 1.0, 0.0).astype(bf16)


def column_places():
    return ones_where(
        (384, 512),
        lambda n: ((n >> 5) & 3) * 96 + (n >> 8) * 48 + ((n >> 4) & 1) * 24 + ((n >> 7) & 1) * 12 + (n & 15),
    )


def row_places():
    return ones_where((96, 128), lambda n: (n >> 6) * 48 + ((n >> 4) & 1) * 24 + ((n >> 5) & 1) * 12 + (n & 15))


def tight():
    return ones_where((384, 512), lambda n: (n >> 4) * 12 + (n & 15))


def order_rows(normed):
    return jnp.concatenate(
        [normed[(il * 3 + ih) * 16 : (il * 3 + ih + 1) * 16] for ih in range(3) for il in range(8)], axis=0
    )


def edge(ordered, w_t):
    projected = nt(w_t, ordered)
    return jax.nn.sigmoid(projected[0:128]) * projected[128:256]


def z_parcel(values, z):
    return jnp.concatenate([values[z * 8 : z * 8 + 8, ih * 128 : ih * 128 + 128] for ih in range(3)], axis=0)


def regroup(parts, roll, bits):
    for zh in range(2):
        for ih in range(3):
            swapped = swap_lanes([parts[zh * 8 + zl][ih * 8 : ih * 8 + 8] for zl in range(8)], 16, roll, bits)
            for il in range(8):
                yield zh, ih, il, swapped[il]


def plain_row(zh, ih, il):
    return zh * 24 + ih * 8 + il


def paired_row(zh, ih, il):
    return (il >> 1) * 12 + (zh * 3 + ih) * 2 + (il & 1)


def assemble(parts, xs):
    return jnp.concatenate(
        [
            jnp.concatenate([parts(x, y * 2 + core) for y in range(4)], axis=1)
            for x in range(xs)
            for core in range(2)
        ],
        axis=0,
    )


def product_out(left, right):
    return nn(nt(left, right).astype(bf16), column_places())


def product_in(left, right, roll):
    rows = []
    for x in range(4):
        for core in range(2):
            rows += swap_lanes([left(x, y * 2 + core).astype(f32) for y in range(4)], 32, roll, (1, 2))
    turned = nt(row_places(), jnp.concatenate(rows, axis=0).astype(bf16)).astype(bf16)
    return nn(nt(turned, tight()).astype(bf16), right)


def unfold(parts, roll):
    columns = [[] for _ in range(8)]
    for ih in range(3):
        turned = jnp.concatenate([part[ih * 8 : ih * 8 + 8] for part in parts], axis=0).T
        for p in range(8):
            columns[p].append(turned[p * 16 : p * 16 + 16])
    return jnp.concatenate(swap_lanes([jnp.concatenate(part, axis=0) for part in columns], 1, roll), axis=0)


def finish(state, combined, gate, weight):
    update = nn(layer_norm(combined).astype(bf16), weight)
    return (state.astype(f32) + gate * update).astype(bf16)


def kernel(
    x_ref, w1_hbm, o1_hbm, w2_hbm, o2_hbm, t1_hbm, t2_hbm, out_ref,
    w1_ref, o1_ref, w2_ref, o2_ref, t1_ref, t2_ref,
    zs, zr, wide, narrow, rs, rr, ls, ll, ls2, ll2, c1s, c1r, c2s, c2r,
    load_sem, z_send, z_recv, r_send, r_recv, l_send, l_recv, l2_send, l2_recv, c1_send, c1_recv, c2_send, c2_recv,
):
    row, col = lax.axis_index("row"), lax.axis_index("col")
    x, zh, core = row // 4, (row // 2) % 2, row % 2
    zl, y = col // 4, col % 4
    z, p = zh * 8 + zl, y * 2 + core
    g = x * 8 + p

    def z_peer(step):
        other = lax.rem(z + step, 16)
        return other, ((x * 2 + other // 8) * 2 + core, lax.rem(other, 8) * 4 + y)

    def g_peer(step):
        dx, dy, dc = step
        other_x, other_y, other_core = lax.rem(x + dx, 4), lax.rem(y + dy, 4), lax.rem(core + dc, 2)
        return (
            other_x * 8 + other_y * 2 + other_core,
            ((other_x * 2 + zh) * 2 + other_core, zl * 4 + other_y),
        )

    barrier = pltpu.get_barrier_semaphore()
    for peer, steps in ((z_peer, Z_STEPS), (g_peer, G_STEPS)):
        for step in steps:
            pl.semaphore_signal(barrier, inc=1, device_id=peer(step)[1], device_id_type=MESH)

    loads = [
        pltpu.make_async_copy(source, target, load_sem.at[i])
        for i, (source, target) in enumerate(
            (
                (w1_hbm, w1_ref), (o1_hbm, o1_ref), (w2_hbm, w2_ref),
                (o2_hbm, o2_ref), (t1_hbm, t1_ref), (t2_hbm, t2_ref),
            )
        )
    ]
    for load in loads:
        load.start()

    sent = []

    def exchange(peer, steps, source, target, me, send, recv):
        for i, step in enumerate(steps):
            other, place = peer(step)
            copy = pltpu.make_async_remote_copy(
                src_ref=source(other), dst_ref=target.at[me], send_sem=send.at[i], recv_sem=recv.at[me],
                device_id=place, device_id_type=MESH,
            )
            copy.start()
            sent.append(copy)

    def arrive(peer, steps, source, target, me, send, recv):
        for i, step in enumerate(steps):
            other, place = peer(step)
            pltpu.make_async_remote_copy(
                src_ref=source(other), dst_ref=target.at[other], send_sem=send.at[i], recv_sem=recv.at[other],
                device_id=place, device_id_type=MESH,
            ).wait_recv()

    def triangle(n, state, w_ref, o_ref):
        normed = layer_norm(state.astype(f32)).astype(bf16)
        ordered = order_rows(normed)
        loads[2 * n].wait()

        def start_z(s):
            values = edge(ordered, w_ref[:, s * 256 : s * 256 + 256].T)
            for other in range(16):
                zs[n, s, other] = z_parcel(values, other).astype(bf16)
            if n == 0 and s == 1:
                pl.semaphore_wait(barrier, len(Z_STEPS) + len(G_STEPS))
            args = (z_peer, Z_STEPS, lambda other: zs.at[n, s, other], zr.at[n, s], z, z_send.at[n, s], z_recv.at[n, s])
            exchange(*args)
            zr[n, s, z] = zs[n, s, z]
            return args

        right_z = start_z(1)
        left_z = start_z(0)
        gate = jax.nn.sigmoid(nn(normed, w_ref[:, 512:640]))
        loads[2 * n + 1].wait()

        arrive(*right_z)
        place_row = (plain_row, paired_row)[n]
        for zh_, ih, il, rows in regroup([zr[n, 1, other].astype(f32) for other in range(16)], roll_lanes, (1, 2, 4)):
            wide[pl.ds(place_row(zh_, ih, il), 8, stride=48), :] = rows
        for c in range(8):
            rs[n, c] = wide[c * 48 : c * 48 + 48, :].astype(bf16)
        right_g = (
            g_peer, G_STEPS, lambda other: rs.at[n, lax.rem(other, 8)], rr.at[n], g, r_send.at[n], r_recv.at[n]
        )
        exchange(*right_g)
        rr[n, g] = rs[n, p]

        arrive(*left_z)
        parts = [zr[n, 0, other].astype(f32) for other in range(16)]
        if n == 0:
            for zh_, ih, il, rows in regroup(parts, roll_lanes, (1, 2, 4)):
                wide[pl.ds(plain_row(zh_, ih, il), 8, stride=48), :] = rows
            for c in range(8):
                ls[c] = wide[c * 48 : c * 48 + 48, :].astype(bf16)
            left_g = (g_peer, P_STEPS, lambda other: ls.at[lax.rem(other, 8)], ll, g, l_send, l_recv)
            exchange(*left_g)
            ll[g] = ls[p]
        else:
            narrow[...] = jnp.zeros_like(narrow)
            for zh_, ih, i, rows in regroup(parts, roll_lanes, (1,)):
                narrow[pl.ds((i >> 1) * 16 + (zh_ * 3 + ih) * 2 + (i & 1), 8, stride=64), :] = rows
            for c in range(8):
                for other in range(4):
                    start = c * 64 + other * 16
                    ls2[c, other] = narrow[start : start + 16, :].astype(bf16)
            left_g = (
                g_peer, G_STEPS, lambda other: ls2.at[lax.rem(other, 8), other // 8], ll2, g, l2_send, l2_recv
            )
            exchange(*left_g)
            ll2[g] = ls2[p, x]
        arrive(*right_g)
        rights = assemble(lambda x_, p_: rr[n, x_ * 8 + p_], 4)
        arrive(*left_g)
        if n == 0:
            total = product_out(assemble(lambda x_, p_: ll[x * 8 + p_], 1), rights)
        else:
            total = product_in(lambda x_, p_: ll2[x_ * 8 + p_], rights, roll_lanes)

        for other in range(8):
            there, far = other % 2, other // 2
            c1s[n, other] = total[there * 48 : there * 48 + 48, far * 128 : far * 128 + 128].astype(bf16)
        c1 = (g_peer, P_STEPS, lambda other: c1s.at[n, lax.rem(other, 8)], c1r.at[n], g, c1_send.at[n], c1_recv.at[n])
        exchange(*c1)
        c1r[n, g] = c1s[n, p]
        arrive(*c1)
        parts = swap_lanes([c1r[n, x * 8 + other].astype(f32) for other in range(8)], 16, roll_lanes)
        for other in range(16):
            half = other // 8
            c2s[n, other] = parts[other % 8][half * 24 : half * 24 + 24].astype(bf16)
        c2 = (z_peer, Z_STEPS, lambda other: c2s.at[n, other], c2r.at[n], z, c2_send.at[n], c2_recv.at[n])
        exchange(*c2)
        c2r[n, z] = c2s[n, z]
        arrive(*c2)
        combined = unfold([c2r[n, other].astype(f32) for other in range(16)], roll_lanes)
        return finish(state, combined, gate, o_ref[...])

    state = x_ref[...].reshape(384, 128)
    state = triangle(0, state, w1_ref, o1_ref)
    state = triangle(1, state, w2_ref, o2_ref)
    normed = layer_norm(state.astype(f32)).astype(bf16)
    loads[4].wait()
    loads[5].wait()
    hidden = nn(normed, t1_ref[...])
    mixed = (jax.nn.silu(hidden[:, :512]) * hidden[:, 512:]).astype(bf16)
    result = (state.astype(f32) + nn(mixed, t2_ref[...])).astype(bf16)
    out_ref[...] = result.reshape(8, 3, 16, 128)
    for copy in sent:
        copy.wait_send()


def body(pair_state, *weights):
    x = jnp.pad(pair_state, ((0, 0), (0, 4), (0, 0))).reshape(3, 8, 16, 128).transpose(1, 0, 2, 3)
    dma = pltpu.SemaphoreType.DMA
    out = pl.pallas_call(
        kernel,
        out_shape=jax.ShapeDtypeStruct((8, 3, 16, 128), bf16),
        in_specs=[pl.BlockSpec(memory_space=pltpu.VMEM)] + [pl.BlockSpec(memory_space=pltpu.HBM)] * 6,
        out_specs=pl.BlockSpec(memory_space=pltpu.VMEM),
        scratch_shapes=[pltpu.VMEM(weight.shape, bf16) for weight in weights]
        + [
            pltpu.VMEM((2, 2, 16, 24, 128), bf16),
            pltpu.VMEM((2, 2, 16, 24, 128), bf16),
            pltpu.VMEM((384, 128), f32),
            pltpu.VMEM((512, 128), f32),
            pltpu.VMEM((2, 8, 48, 128), bf16),
            pltpu.VMEM((2, 32, 48, 128), bf16),
            pltpu.VMEM((8, 48, 128), bf16),
            pltpu.VMEM((32, 48, 128), bf16),
            pltpu.VMEM((8, 4, 16, 128), bf16),
            pltpu.VMEM((32, 16, 128), bf16),
            pltpu.VMEM((2, 8, 48, 128), bf16),
            pltpu.VMEM((2, 32, 48, 128), bf16),
            pltpu.VMEM((2, 16, 24, 128), bf16),
            pltpu.VMEM((2, 16, 24, 128), bf16),
            dma((6,)),
            dma((2, 2, 16)), dma((2, 2, 16)),
            dma((2, 32)), dma((2, 32)),
            dma((8,)), dma((32,)),
            dma((32,)), dma((32,)),
            dma((2, 8)), dma((2, 32)),
            dma((2, 16)), dma((2, 16)),
        ],
        compiler_params=pltpu.CompilerParams(
            collective_id=0, has_side_effects=True, vmem_limit_bytes=48 * 2**20
        ),
    )(x, *weights)
    return out.transpose(1, 0, 2, 3).reshape(24, 16, 128)[:, :12]


def solution(mesh):
    placed = (P("row", "col", None), P(), P(), P(), P(), P(), P())
    return jax.shard_map(
        body, mesh=mesh, in_specs=placed, out_specs=P("row", "col", None), check_vma=False
    )
```

time: 101 us -> 86.1 us (0.85)
  Pallas kernels: 95.4 us -> 80.7 us
    pallas_call x1, Pallas kernels: 95.4 us -> 80.7 us  [body(): pl.pallas_call(kernel, out_shape=jax.ShapeDtypeStruct((8, 3, 16, 128), bf...]
where the time goes in v2:
time: 86.1 us; the launch traced here: 85.7 us
  Pallas kernels  80.7 us (94%)
  local copies, waits for them, and re-layouts  4.99 us (6%)
    pallas_call x1, Pallas kernels, body(): pl.pallas_call(kernel, out_shape=jax.ShapeDtypeStruct((8, 3, 16, 128), bf...  80.7 us
    unnamed x13, local copies, waits for them, and re-layouts  4.3 us

profile of v2, /device:TPU:1, one launch (start us, length us, event | category | flops | bytes accessed | tf_op | source)
XLA Modules:
  0.0 85.7 jit_solution(1114697334285376613)
XLA Ops:
  0.0 0.0 copy-start
  0.0 0.9 %copy.8 = bf16[24,12,128]{2,1,0:T(8,128)(2,1)S(1)} copy(bf16[24,12,128]{2,0,1:T(8,128)(2,1)} %param.7) | data formatting | bytes 147456 | tf_op args[0]
  1.0 0.0 copy-start.1
  1.0 0.0 copy-start.3
  1.0 0.0 copy-done
  1.0 0.8 copy-done.1
  1.9 0.1 copy-done.3
  1.9 0.0 copy-start.2
  1.9 0.9 %copy-done.2 = bf16[128,640]{1,0:T(8,128)(2,1)S(1)} copy-done((bf16[128,640]{1,0:T(8,128)(2,1)S(1)}, bf16[128,640]{1,0:T(8,128)(2,1)}, u32[]{:S(2)}) %copy-start.2) | copy-done | bytes 163864
  2.9 0.0 copy-start.4
  2.9 0.8 copy-done.4
  3.6 0.0 copy-start.5
  3.6 0.8 copy-done.5
  4.4 80.7 %shard_map.73 = bf16[8,3,16,128]{3,2,1,0:T(8,128)(2,1)S(1)} custom-call(bf16[8,3,16,128]{3,2,1,0:T(8,128)(2,1)S(1)} %bitcast.7, bf16[128,640]{1,0:T(8,128)(2,1)S(1)} %copy-done.1, bf16[128,128]{1,0:T(8,128)(2,1)S(1)} %copy-done.4, bf16[128,640]{1,0:T(8,128)(2,1)S(1)} %copy-done.2, bf16[128,128]{1,0:T(8,128)(2,1)S(1)} %copy-done.5, ...), custom_call_target="tpu_custom_call" | custom-call | tf_op jit(solution)/shard_map/pallas_call | solution.py:305
  85.1 0.7 copy.11
  (3 shorter events, 0.0 us)
Async XLA Ops:
  0.0 1.0 %copy-start = (bf16[128,1024]{1,0:T(8,128)(2,1)S(1)}, bf16[128,1024]{1,0:T(8,128)(2,1)}, u32[]{:S(2)}) copy-start(bf16[128,1024]{1,0:T(8,128)(2,1)} %t1_hbm.1) | copy-start | bytes 786436
  1.0 0.9 %copy-start.1 = (bf16[128,640]{1,0:T(8,128)(2,1)S(1)}, bf16[128,640]{1,0:T(8,128)(2,1)}, u32[]{:S(2)}) copy-start(bf16[128,640]{1,0:T(8,128)(2,1)} %w1_hbm.1) | copy-start | bytes 491524
  1.0 1.0 %copy-start.3 = (bf16[512,128]{1,0:T(8,128)(2,1)S(1)}, bf16[512,128]{1,0:T(8,128)(2,1)}, u32[]{:S(2)}) copy-start(bf16[512,128]{1,0:T(8,128)(2,1)} %t2_hbm.1) | copy-start | bytes 393220
  1.9 0.9 %copy-start.2 = (bf16[128,640]{1,0:T(8,128)(2,1)S(1)}, bf16[128,640]{1,0:T(8,128)(2,1)}, u32[]{:S(2)}) copy-start(bf16[128,640]{1,0:T(8,128)(2,1)} %w2_hbm.1) | copy-start | bytes 491524
  2.9 0.8 copy-start.4
  3.6 0.8 copy-start.5

commit v3 on v2

v3 whole, which is shorter than its diff:
```python
import jax
import jax.numpy as jnp
from jax import lax
from jax.experimental import pallas as pl
from jax.experimental.pallas import tpu as pltpu
from jax.sharding import PartitionSpec as P

MESH = pl.DeviceIdType.MESH
norm_eps = 1e-05
f32 = jnp.float32
bf16 = jnp.bfloat16

Z_STEPS = (8, 7, 9, 6, 10, 5, 11, 4, 12, 3, 13, 2, 14, 1, 15)
RING = (2, 1, 3, 0)
P_STEPS = tuple((0, dy, dc) for dy in RING for dc in (1, 0) if (dy, dc) != (0, 0))
G_STEPS = tuple(
    sorted(
        ((dx, dy, dc) for dx in RING for dy in RING for dc in (1, 0) if (dx, dy, dc) != (0, 0, 0)),
        key=lambda step: -(min(step[0], 4 - step[0]) + min(step[1], 4 - step[1])),
    )
)


def roll_lanes(values, shift):
    return pltpu.roll(values, shift, 1)


def swap_lanes(parts, width, roll, bits=(1, 2, 4)):
    lane = lax.broadcasted_iota(jnp.int32, parts[0].shape, 1)
    parts = list(parts)
    for bit in bits:
        low = (lane & (bit * width)) == 0
        for a in range(len(parts)):
            if a & bit == 0:
                first, second = parts[a], parts[a | bit]
                parts[a] = jnp.where(low, first, roll(second, bit * width))
                parts[a | bit] = jnp.where(low, roll(first, 128 - bit * width), second)
    return parts


def layer_norm(values):
    centred = values - jnp.mean(values, axis=-1, keepdims=True)
    spread = jnp.mean(centred * centred, axis=-1, keepdims=True)
    return centred * lax.rsqrt(spread + norm_eps)


def nt(a, b):
    return lax.dot_general(a, b, (((1,), (1,)), ((), ())), preferred_element_type=f32)


def nn(a, b):
    return jnp.dot(a, b, preferred_element_type=f32)


def ones_where(shape, row_of):
    row = lax.broadcasted_iota(jnp.int32, shape, 0)
    column = lax.broadcasted_iota(jnp.int32, shape, 1)
    return jnp.where((row == row_of(column)) & ((column & 15) < 12), 1.0, 0.0).astype(bf16)


def column_places():
    return ones_where(
        (384, 512),
        lambda n: ((n >> 5) & 3) * 96 + (n >> 8) * 48 + ((n >> 4) & 1) * 24 + ((n >> 7) & 1) * 12 + (n & 15),
    )


def row_places():
    return ones_where((96, 128), lambda n: (n >> 6) * 48 + ((n >> 4) & 1) * 24 + ((n >> 5) & 1) * 12 + (n & 15))


def order_rows(normed):
    return jnp.concatenate(
        [normed[(il * 3 + ih) * 16 : (il * 3 + ih + 1) * 16] for ih in range(3) for il in range(8)], axis=0
    )


def edge(ordered, w_t):
    projected = nt(w_t, ordered)
    return jax.nn.sigmoid(projected[0:128]) * projected[128:256]


def z_parcel(values, z):
    return jnp.concatenate([values[z * 8 : z * 8 + 8, ih * 128 : ih * 128 + 128] for ih in range(3)], axis=0)


def regroup(parts, roll):
    for ih in range(3):
        swapped = swap_lanes([part[ih * 8 : ih * 8 + 8] for part in parts], 16, roll)
        for il in range(8):
            yield ih * 8 + il, swapped[il]


def assemble(parts):
    return jnp.concatenate(
        [
            jnp.concatenate([parts(x, y * 2 + core, zh) for y in range(4)], axis=1)
            for x in range(4)
            for core in range(2)
            for zh in range(2)
        ],
        axis=0,
    )


def slot_is_remote(from_x, from_z, x, z):
    return jnp.logical_or(from_z != z, x != from_x)


def product_out(left, right, places):
    return nn(nt(left, right).astype(bf16), places)


def product_in(left, right, places, roll):
    cores = [swap_lanes([left(y * 2 + core).astype(f32) for y in range(4)], 32, roll, (1, 2)) for core in range(2)]
    rows = jnp.concatenate([cores[core][x] for x in range(4) for core in range(2)], axis=0)
    return nn(nt(places, rows.astype(bf16)).astype(bf16), right)


def unfold(parts, roll):
    columns = [[] for _ in range(8)]
    for ih in range(3):
        turned = jnp.concatenate([part[ih * 8 : ih * 8 + 8] for part in parts], axis=0).T
        for p in range(8):
            columns[p].append(turned[p * 16 : p * 16 + 16])
    return jnp.concatenate(swap_lanes([jnp.concatenate(part, axis=0) for part in columns], 1, roll), axis=0)


def finish(state, combined, gate, weight):
    update = nn(layer_norm(combined).astype(bf16), weight)
    return (state.astype(f32) + gate * update).astype(bf16)


def kernel(
    x_hbm, w1_hbm, o1_hbm, w2_hbm, o2_hbm, t1_hbm, t2_hbm, out_ref,
    x_ref, w1_ref, o1_ref, w2_ref, o2_ref, t1_ref, t2_ref,
    block, columns, rows, zs, zr, half, wide, rs, rr, ls, ll, c1s, c1r, c2s, c2r,
    load_sem, z_send, z_recv, r_send, r_recv, l_send, l_recv, c1_send, c1_recv, c2_send, c2_recv,
):
    row, col = lax.axis_index("row"), lax.axis_index("col")
    x, zh, core = row // 4, (row // 2) % 2, row % 2
    zl, y = col // 4, col % 4
    z, p = zh * 8 + zl, y * 2 + core
    g = x * 8 + p
    far_x = zl // 2

    def z_place(at_x, at_z):
        return ((at_x * 2 + at_z // 8) * 2 + core, lax.rem(at_z, 8) * 4 + y)

    def z_peer(step):
        other = lax.rem(z + step, 16)
        return other, z_place(x, other)

    def g_peer(step):
        dx, dy, dc = step
        other_x, other_y, other_core = lax.rem(x + dx, 4), lax.rem(y + dy, 4), lax.rem(core + dc, 2)
        return (
            other_x * 8 + other_y * 2 + other_core,
            ((other_x * 2 + zh) * 2 + other_core, zl * 4 + other_y),
        )

    def load(i, source, target):
        copy = pltpu.make_async_copy(source, target, load_sem.at[i])
        copy.start()
        return copy

    first_loads = [load(0, x_hbm, x_ref), load(1, w1_hbm, w1_ref)]

    barrier = pltpu.get_barrier_semaphore()
    for step in Z_STEPS:
        pl.semaphore_signal(barrier, inc=1, device_id=z_peer(step)[1], device_id_type=MESH)
    for dx in (2, 1, 3):
        for source in range(4):
            at_z = (source // 2) * 8 + x * 2 + source % 2
            pl.semaphore_signal(
                barrier, inc=1, device_id=z_place(lax.rem(x + dx, 4), at_z), device_id_type=MESH
            )
    for step in G_STEPS:
        pl.semaphore_signal(barrier, inc=1, device_id=g_peer(step)[1], device_id_type=MESH)
    greeted = len(Z_STEPS) + len(G_STEPS) + jnp.where(far_x == x, 0, 16)

    columns[...] = column_places()
    rows[...] = row_places()
    block[...] = jnp.zeros_like(block)

    sent = []

    def exchange(peer, steps, source, target, me, send, recv):
        for i, step in enumerate(steps):
            other, place = peer(step)
            copy = pltpu.make_async_remote_copy(
                src_ref=source(other), dst_ref=target(me), send_sem=send.at[i], recv_sem=recv.at[me],
                device_id=place, device_id_type=MESH,
            )
            copy.start()
            sent.append(copy)

    def arrive(peer, steps, source, target, me, send, recv):
        for i, step in enumerate(steps):
            other, place = peer(step)
            pltpu.make_async_remote_copy(
                src_ref=source(other), dst_ref=target(other), send_sem=send.at[i], recv_sem=recv.at[other],
                device_id=place, device_id_type=MESH,
            ).wait_recv()

    def far_copy(step, target, recv):
        other = lax.rem(z + step, 16)
        return pltpu.make_async_remote_copy(
            src_ref=zs.at[1, 0, other], dst_ref=zr.at[1, 0, target], send_sem=z_send.at[1, 0, step],
            recv_sem=z_recv.at[1, 0, recv], device_id=z_place(far_x, other), device_id_type=MESH,
        )

    def triangle(n, state, w_ref, o_ref, w_load, o_load):
        normed = layer_norm(state.astype(f32)).astype(bf16)
        ordered = order_rows(normed)
        w_load.wait()

        def fill_z(s):
            values = edge(ordered, w_ref[:, s * 256 : s * 256 + 256].T)
            for other in range(16):
                zs[n, s, other] = z_parcel(values, other).astype(bf16)
            return (
                z_peer, Z_STEPS, lambda other: zs.at[n, s, other], lambda me: zr.at[n, s, me], z,
                z_send.at[n, s], z_recv.at[n, s],
            )

        right_z = fill_z(1)
        if n == 0:
            pl.semaphore_wait(barrier, greeted)
        exchange(*right_z)
        zr[n, 1, z] = zs[n, 1, z]
        left_z = fill_z(0)
        slot = x * 4 + zh * 2 + lax.rem(zl, 2)
        if n == 0:
            exchange(*left_z)
            zr[n, 0, z] = zs[n, 0, z]
        else:
            for step in Z_STEPS:
                far_copy(step, slot, slot).start()

            @pl.when(far_x != x)
            def _():
                far_copy(0, slot, slot).start()

            @pl.when(far_x == x)
            def _():
                zr[1, 0, slot] = zs[1, 0, z]

        gate = jax.nn.sigmoid(nn(normed, w_ref[:, 512:640]))

        for part in range(2):
            there = zh if part == 0 else 1 - zh
            base = there * 8
            for other in range(8):

                @pl.when(base + other != z)
                def _():
                    pltpu.make_async_remote_copy(
                        src_ref=zs.at[n, 1, other], dst_ref=zr.at[n, 1, base + other], send_sem=z_send.at[n, 1, 0],
                        recv_sem=z_recv.at[n, 1, base + other], device_id=z_place(x, base + other),
                        device_id_type=MESH,
                    ).wait_recv()

            for i, values in regroup([zr[n, 1, base + other].astype(f32) for other in range(8)], roll_lanes):
                half[pl.ds(i, 8, stride=24), :] = values
            for c in range(8):
                rs[n, part, c] = half[c * 24 : c * 24 + 24, :].astype(bf16)
            exchange(
                g_peer, G_STEPS, lambda other: rs.at[n, part, lax.rem(other, 8)], lambda me: rr.at[n, there, me], g,
                r_send.at[n, part], r_recv.at[n, there],
            )
            rr[n, there, g] = rs[n, part, p]

        if n == 0:
            arrive(*left_z)
            parts = [[zr[n, 0, zh_ * 8 + zl_].astype(f32) for zl_ in range(8)] for zh_ in range(2)]
        else:
            for other in range(16):
                at_z = ((other // 2) % 2) * 8 + x * 2 + other % 2

                @pl.when(slot_is_remote(other // 4, at_z, x, z))
                def _():
                    far_copy(0, other, other).wait_recv()

            parts = [
                [zr[n, 0, x_ * 4 + zh_ * 2 + zlo].astype(f32) for x_ in range(4) for zlo in range(2)]
                for zh_ in range(2)
            ]
        for zh_ in range(2):
            for i, values in regroup(parts[zh_], roll_lanes):
                wide[pl.ds(zh_ * 24 + i, 8, stride=48), :] = values
        for c in range(8):
            ls[n, c] = wide[c * 48 : c * 48 + 48, :].astype(bf16)
        left_g = (
            g_peer, P_STEPS, lambda other: ls.at[n, lax.rem(other, 8)], lambda me: ll.at[n, me], g,
            l_send.at[n], l_recv.at[n],
        )
        exchange(*left_g)
        ll[n, g] = ls[n, p]
        for there in range(2):
            arrive(
                g_peer, G_STEPS, lambda other: rs.at[n, 0, lax.rem(other, 8)], lambda me: rr.at[n, there, me], g,
                r_send.at[n, 0], r_recv.at[n, there],
            )
        rights = assemble(lambda x_, p_, zh_: rr[n, zh_, x_ * 8 + p_])
        arrive(*left_g)
        if n == 0:
            lefts = jnp.concatenate(
                [
                    jnp.concatenate([ll[n, x * 8 + y_ * 2 + core_] for y_ in range(4)], axis=1)
                    for core_ in range(2)
                ],
                axis=0,
            )
            total = product_out(lefts, rights, columns[...])
        else:
            total = product_in(lambda p_: ll[n, x * 8 + p_], rights, rows[...], roll_lanes)

        for other in range(8):
            there, far = other % 2, other // 2
            c1s[n, other] = total[there * 48 : there * 48 + 48, far * 128 : far * 128 + 128].astype(bf16)
        c1 = (
            g_peer, P_STEPS, lambda other: c1s.at[n, lax.rem(other, 8)], lambda me: c1r.at[n, me], g,
            c1_send.at[n], c1_recv.at[n],
        )
        exchange(*c1)
        c1r[n, g] = c1s[n, p]
        arrive(*c1)
        parts = swap_lanes([c1r[n, x * 8 + other].astype(f32) for other in range(8)], 16, roll_lanes)
        for other in range(16):
            start = (other // 8) * 24
            c2s[n, other] = parts[other % 8][start : start + 24].astype(bf16)
        c2 = (
            z_peer, Z_STEPS, lambda other: c2s.at[n, other], lambda me: c2r.at[n, me], z,
            c2_send.at[n], c2_recv.at[n],
        )
        exchange(*c2)
        c2r[n, z] = c2s[n, z]
        o_load.wait()
        arrive(*c2)
        combined = unfold([c2r[n, other].astype(f32) for other in range(16)], roll_lanes)
        return finish(state, combined, gate, o_ref[...])

    first_loads[0].wait()
    for k in range(12):
        for ih in range(3):
            block[pl.ds(ih * 16 + k, 8, stride=48), :] = x_ref[k, ih * 8 : ih * 8 + 8].astype(f32)
    later = [
        load(2 + i, source, target)
        for i, (source, target) in enumerate(
            ((o1_hbm, o1_ref), (w2_hbm, w2_ref), (o2_hbm, o2_ref), (t1_hbm, t1_ref), (t2_hbm, t2_ref))
        )
    ]
    state = block[...].astype(bf16)
    state = triangle(0, state, w1_ref, o1_ref, first_loads[1], later[0])
    state = triangle(1, state, w2_ref, o2_ref, later[1], later[2])
    normed = layer_norm(state.astype(f32)).astype(bf16)
    later[3].wait()
    later[4].wait()
    hidden = nn(normed, t1_ref[...])
    mixed = (jax.nn.silu(hidden[:, :512]) * hidden[:, 512:]).astype(bf16)
    block[...] = state.astype(f32) + nn(mixed, t2_ref[...])
    for k in range(12):
        out_ref[k] = jnp.concatenate(
            [block[pl.ds(ih * 16 + k, 8, stride=48), :] for ih in range(3)], axis=0
        ).astype(bf16)
    for copy in sent:
        copy.wait_send()
    for step in Z_STEPS:
        far_copy(step, 0, 0).wait_send()

    @pl.when(far_x != x)
    def _():
        far_copy(0, 0, 0).wait_send()


def body(pair_state, *weights):
    dma = pltpu.SemaphoreType.DMA
    out = pl.pallas_call(
        kernel,
        out_shape=jax.ShapeDtypeStruct((12, 24, 128), bf16),
        in_specs=[pl.BlockSpec(memory_space=pltpu.HBM)] * 7,
        out_specs=pl.BlockSpec(memory_space=pltpu.VMEM),
        scratch_shapes=[pltpu.VMEM((12, 24, 128), bf16)]
        + [pltpu.VMEM(weight.shape, bf16) for weight in weights]
        + [
            pltpu.VMEM((384, 128), f32),
            pltpu.VMEM((384, 512), bf16),
            pltpu.VMEM((96, 128), bf16),
            pltpu.VMEM((2, 2, 16, 24, 128), bf16),
            pltpu.VMEM((2, 2, 16, 24, 128), bf16),
            pltpu.VMEM((192, 128), f32),
            pltpu.VMEM((384, 128), f32),
            pltpu.VMEM((2, 2, 8, 24, 128), bf16),
            pltpu.VMEM((2, 2, 32, 24, 128), bf16),
            pltpu.VMEM((2, 8, 48, 128), bf16),
            pltpu.VMEM((2, 32, 48, 128), bf16),
            pltpu.VMEM((2, 8, 48, 128), bf16),
            pltpu.VMEM((2, 32, 48, 128), bf16),
            pltpu.VMEM((2, 16, 24, 128), bf16),
            pltpu.VMEM((2, 16, 24, 128), bf16),
            dma((7,)),
            dma((2, 2, 16)), dma((2, 2, 16)),
            dma((2, 2, 32)), dma((2, 2, 32)),
            dma((2, 8)), dma((2, 32)),
            dma((2, 8)), dma((2, 32)),
            dma((2, 16)), dma((2, 16)),
        ],
        compiler_params=pltpu.CompilerParams(
            collective_id=0, has_side_effects=True, vmem_limit_bytes=60 * 2**20
        ),
    )(pair_state.transpose(1, 0, 2), *weights)
    return out.transpose(1, 0, 2)


def solution(mesh):
    placed = (P("row", "col", None), P(), P(), P(), P(), P(), P())
    return jax.shard_map(
        body, mesh=mesh, in_specs=placed, out_specs=P("row", "col", None), check_vma=False
    )
```

time: 86.1 us -> 85 us (0.987); the launches traced: 85.7 us -> 83.7 us
  local copies, waits for them, and re-layouts: 4.99 us -> 1.52 us
  Pallas kernels: 80.7 us -> 82.2 us
    unnamed x13 -> x1, local copies, waits for them, and re-layouts: 4.3 us -> 1.52 us
    pallas_call x1, Pallas kernels: 80.7 us -> 82.2 us  [body(): pl.pallas_call(kernel, out_shape=jax.ShapeDtypeStruct((12, 24, 128), bf16...]
where the time goes in v3:
time: 85 us; the launch traced here: 83.7 us
  Pallas kernels  82.2 us (97%)
  local copies, waits for them, and re-layouts  1.52 us (2%)
    pallas_call x1, Pallas kernels, body(): pl.pallas_call(kernel, out_shape=jax.ShapeDtypeStruct((12, 24, 128), bf16...  82.2 us

profile of v3, /device:TPU:1, one launch (start us, length us, event | category | flops | bytes accessed | tf_op | source)
XLA Modules:
  0.0 83.7 jit_solution(4265795264052480029)
XLA Ops:
  0.0 82.2 %shard_map.73 = bf16[12,24,128]{2,1,0:T(8,128)(2,1)} custom-call(bf16[12,24,128]{2,1,0:T(8,128)(2,1)} %bitcast.3, bf16[128,640]{1,0:T(8,128)(2,1)} %w1_hbm.1, bf16[128,128]{1,0:T(8,128)(2,1)} %o1_hbm.1, bf16[128,640]{1,0:T(8,128)(2,1)} %w2_hbm.1, bf16[128,128]{1,0:T(8,128)(2,1)} %o2_hbm.1, bf16[128,1024]{1,0:T(8,128)(2,1)} %t1_hbm.1, bf16[512,128]{1,0:T(8,128)(2,1)} %t2_hbm.1), custom_call_target="tpu_custom_call" | custom-call | tf_op jit(solution)/shard_map/pallas_call | solution.py:379
  82.2 1.5 %copy.9 = bf16[24,12,128]{2,0,1:T(8,128)(2,1)} copy(bf16[24,12,128]{2,0,1:T(8,128)(2,1)} %bitcast.2) | data formatting | bytes 147456

commit v4 on v3

--- a/solution.py
+++ b/solution.py
@@ -94,17 +94,12 @@
 def assemble(parts):
     return jnp.concatenate(
         [
-            jnp.concatenate([parts(x, y * 2 + core, zh) for y in range(4)], axis=1)
+            jnp.concatenate([parts(x, y * 2 + core) for y in range(4)], axis=1)
             for x in range(4)
             for core in range(2)
-            for zh in range(2)
         ],
         axis=0,
     )
-
-
-def slot_is_remote(from_x, from_z, x, z):
-    return jnp.logical_or(from_z != z, x != from_x)
 
 
 def product_out(left, right, places):
@@ -134,7 +129,7 @@
 def kernel(
     x_hbm, w1_hbm, o1_hbm, w2_hbm, o2_hbm, t1_hbm, t2_hbm, out_ref,
     x_ref, w1_ref, o1_ref, w2_ref, o2_ref, t1_ref, t2_ref,
-    block, columns, rows, zs, zr, half, wide, rs, rr, ls, ll, c1s, c1r, c2s, c2r,
+    block, columns, rows, zs, zr, wide, rs, rr, ls, ll, c1s, c1r, c2s, c2r,
     load_sem, z_send, z_recv, r_send, r_recv, l_send, l_recv, c1_send, c1_recv, c2_send, c2_recv,
 ):
     row, col = lax.axis_index("row"), lax.axis_index("col")
@@ -143,6 +138,7 @@
     z, p = zh * 8 + zl, y * 2 + core
     g = x * 8 + p
     far_x = zl // 2
+    from_own = far_x == x
 
     def z_place(at_x, at_z):
         return ((at_x * 2 + at_z // 8) * 2 + core, lax.rem(at_z, 8) * 4 + y)
@@ -177,7 +173,7 @@
             )
     for step in G_STEPS:
         pl.semaphore_signal(barrier, inc=1, device_id=g_peer(step)[1], device_id_type=MESH)
-    greeted = len(Z_STEPS) + len(G_STEPS) + jnp.where(far_x == x, 0, 16)
+    greeted = len(Z_STEPS) + len(G_STEPS) + jnp.where(from_own, 0, 16)
 
     columns[...] = column_places()
     rows[...] = row_places()
@@ -186,41 +182,42 @@
     sent = []
 
     def exchange(peer, steps, source, target, me, send, recv):
-        for i, step in enumerate(steps):
-            other, place = peer(step)
-            copy = pltpu.make_async_remote_copy(
-                src_ref=source(other), dst_ref=target(me), send_sem=send.at[i], recv_sem=recv.at[me],
-                device_id=place, device_id_type=MESH,
-            )
-            copy.start()
-            sent.append(copy)
-
-    def arrive(peer, steps, source, target, me, send, recv):
-        for i, step in enumerate(steps):
+        for step in steps:
             other, place = peer(step)
             pltpu.make_async_remote_copy(
-                src_ref=source(other), dst_ref=target(other), send_sem=send.at[i], recv_sem=recv.at[other],
+                src_ref=source(other), dst_ref=target.at[me], send_sem=send, recv_sem=recv,
                 device_id=place, device_id_type=MESH,
-            ).wait_recv()
-
-    def far_copy(step, target, recv):
+            ).start()
+        sent.append((target, len(steps), send))
+
+    def all_bytes(target, count, sem):
+        blocks = target.at[pl.ds(0, count)]
+        return pltpu.make_async_copy(blocks, blocks, sem)
+
+    def arrive(peer, steps, source, target, me, send, recv):
+        all_bytes(target, len(steps), recv).wait()
+
+    def far_copy(step):
         other = lax.rem(z + step, 16)
-        return pltpu.make_async_remote_copy(
-            src_ref=zs.at[1, 0, other], dst_ref=zr.at[1, 0, target], send_sem=z_send.at[1, 0, step],
-            recv_sem=z_recv.at[1, 0, recv], device_id=z_place(far_x, other), device_id_type=MESH,
-        )
-
-    def triangle(n, state, w_ref, o_ref, w_load, o_load):
+        pltpu.make_async_remote_copy(
+            src_ref=zs.at[1, 0, other], dst_ref=zr.at[1, 0, x * 4 + zh * 2 + lax.rem(zl, 2)],
+            send_sem=z_send.at[1, 0], recv_sem=z_recv.at[1, 0],
+            device_id=z_place(far_x, other), device_id_type=MESH,
+        ).start()
+
+    later = []
+
+    def triangle(n, state, w_ref, o_ref):
         normed = layer_norm(state.astype(f32)).astype(bf16)
         ordered = order_rows(normed)
-        w_load.wait()
+        (first_loads[1] if n == 0 else later[1]).wait()
 
         def fill_z(s):
             values = edge(ordered, w_ref[:, s * 256 : s * 256 + 256].T)
             for other in range(16):
                 zs[n, s, other] = z_parcel(values, other).astype(bf16)
             return (
-                z_peer, Z_STEPS, lambda other: zs.at[n, s, other], lambda me: zr.at[n, s, me], z,
+                z_peer, Z_STEPS, lambda other: zs.at[n, s, other], zr.at[n, s], z,
                 z_send.at[n, s], z_recv.at[n, s],
             )
 
@@ -234,53 +231,48 @@
         if n == 0:
             exchange(*left_z)
             zr[n, 0, z] = zs[n, 0, z]
+            for i, (source, target) in enumerate(
+                ((o1_hbm, o1_ref), (w2_hbm, w2_ref), (o2_hbm, o2_ref), (t1_hbm, t1_ref), (t2_hbm, t2_ref))
+            ):
+                later.append(load(2 + i, source, target))
         else:
             for step in Z_STEPS:
-                far_copy(step, slot, slot).start()
-
-            @pl.when(far_x != x)
+                far_copy(step)
+
+            @pl.when(jnp.logical_not(from_own))
             def _():
-                far_copy(0, slot, slot).start()
-
-            @pl.when(far_x == x)
+                far_copy(0)
+
+            @pl.when(from_own)
             def _():
                 zr[1, 0, slot] = zs[1, 0, z]
 
         gate = jax.nn.sigmoid(nn(normed, w_ref[:, 512:640]))
 
-        for part in range(2):
-            there = zh if part == 0 else 1 - zh
-            base = there * 8
-            for other in range(8):
-
-                @pl.when(base + other != z)
-                def _():
-                    pltpu.make_async_remote_copy(
-                        src_ref=zs.at[n, 1, other], dst_ref=zr.at[n, 1, base + other], send_sem=z_send.at[n, 1, 0],
-                        recv_sem=z_recv.at[n, 1, base + other], device_id=z_place(x, base + other),
-                        device_id_type=MESH,
-                    ).wait_recv()
-
-            for i, values in regroup([zr[n, 1, base + other].astype(f32) for other in range(8)], roll_lanes):
-                half[pl.ds(i, 8, stride=24), :] = values
-            for c in range(8):
-                rs[n, part, c] = half[c * 24 : c * 24 + 24, :].astype(bf16)
-            exchange(
-                g_peer, G_STEPS, lambda other: rs.at[n, part, lax.rem(other, 8)], lambda me: rr.at[n, there, me], g,
-                r_send.at[n, part], r_recv.at[n, there],
-            )
-            rr[n, there, g] = rs[n, part, p]
+        arrive(*right_z)
+        for zh_ in range(2):
+            for i, values in regroup([zr[n, 1, zh_ * 8 + zl_].astype(f32) for zl_ in range(8)], roll_lanes):
+                wide[pl.ds(zh_ * 24 + i, 8, stride=48), :] = values
+        for c in range(8):
+            rs[n, c] = wide[c * 48 : c * 48 + 48, :].astype(bf16)
+        right_g = (
+            g_peer, G_STEPS, lambda other: rs.at[n, lax.rem(other, 8)], rr.at[n], g,
+            r_send.at[n], r_recv.at[n],
+        )
+        exchange(*right_g)
+        rr[n, g] = rs[n, p]
 
         if n == 0:
             arrive(*left_z)
             parts = [[zr[n, 0, zh_ * 8 + zl_].astype(f32) for zl_ in range(8)] for zh_ in range(2)]
         else:
-            for other in range(16):
-                at_z = ((other // 2) % 2) * 8 + x * 2 + other % 2
-
-                @pl.when(slot_is_remote(other // 4, at_z, x, z))
-                def _():
-                    far_copy(0, other, other).wait_recv()
+            @pl.when(from_own)
+            def _():
+                all_bytes(zr.at[1, 0], 15, z_recv.at[1, 0]).wait()
+
+            @pl.when(jnp.logical_not(from_own))
+            def _():
+                all_bytes(zr.at[1, 0], 16, z_recv.at[1, 0]).wait()
 
             parts = [
                 [zr[n, 0, x_ * 4 + zh_ * 2 + zlo].astype(f32) for x_ in range(4) for zlo in range(2)]
@@ -292,17 +284,13 @@
         for c in range(8):
             ls[n, c] = wide[c * 48 : c * 48 + 48, :].astype(bf16)
         left_g = (
-            g_peer, P_STEPS, lambda other: ls.at[n, lax.rem(other, 8)], lambda me: ll.at[n, me], g,
+            g_peer, P_STEPS, lambda other: ls.at[n, lax.rem(other, 8)], ll.at[n], g,
             l_send.at[n], l_recv.at[n],
         )
         exchange(*left_g)
         ll[n, g] = ls[n, p]
-        for there in range(2):
-            arrive(
-                g_peer, G_STEPS, lambda other: rs.at[n, 0, lax.rem(other, 8)], lambda me: rr.at[n, there, me], g,
-                r_send.at[n, 0], r_recv.at[n, there],
-            )
-        rights = assemble(lambda x_, p_, zh_: rr[n, zh_, x_ * 8 + p_])
+        arrive(*right_g)
+        rights = assemble(lambda x_, p_: rr[n, x_ * 8 + p_])
         arrive(*left_g)
         if n == 0:
             lefts = jnp.concatenate(
@@ -320,7 +308,7 @@
             there, far = other % 2, other // 2
             c1s[n, other] = total[there * 48 : there * 48 + 48, far * 128 : far * 128 + 128].astype(bf16)
         c1 = (
-            g_peer, P_STEPS, lambda other: c1s.at[n, lax.rem(other, 8)], lambda me: c1r.at[n, me], g,
+            g_peer, P_STEPS, lambda other: c1s.at[n, lax.rem(other, 8)], c1r.at[n], g,
             c1_send.at[n], c1_recv.at[n],
         )
         exchange(*c1)
@@ -331,12 +319,12 @@
             start = (other // 8) * 24
             c2s[n, other] = parts[other % 8][start : start + 24].astype(bf16)
         c2 = (
-            z_peer, Z_STEPS, lambda other: c2s.at[n, other], lambda me: c2r.at[n, me], z,
+            z_peer, Z_STEPS, lambda other: c2s.at[n, other], c2r.at[n], z,
             c2_send.at[n], c2_recv.at[n],
         )
         exchange(*c2)
         c2r[n, z] = c2s[n, z]
-        o_load.wait()
+        later[2 * n].wait()
         arrive(*c2)
         combined = unfold([c2r[n, other].astype(f32) for other in range(16)], roll_lanes)
         return finish(state, combined, gate, o_ref[...])
@@ -345,15 +333,9 @@
     for k in range(12):
         for ih in range(3):
             block[pl.ds(ih * 16 + k, 8, stride=48), :] = x_ref[k, ih * 8 : ih * 8 + 8].astype(f32)
-    later = [
-        load(2 + i, source, target)
-        for i, (source, target) in enumerate(
-            ((o1_hbm, o1_ref), (w2_hbm, w2_ref), (o2_hbm, o2_ref), (t1_hbm, t1_ref), (t2_hbm, t2_ref))
-        )
-    ]
     state = block[...].astype(bf16)
-    state = triangle(0, state, w1_ref, o1_ref, first_loads[1], later[0])
-    state = triangle(1, state, w2_ref, o2_ref, later[1], later[2])
+    state = triangle(0, state, w1_ref, o1_ref)
+    state = triangle(1, state, w2_ref, o2_ref)
     normed = layer_norm(state.astype(f32)).astype(bf16)
     later[3].wait()
     later[4].wait()
@@ -364,14 +346,16 @@
         out_ref[k] = jnp.concatenate(
             [block[pl.ds(ih * 16 + k, 8, stride=48), :] for ih in range(3)], axis=0
         ).astype(bf16)
-    for copy in sent:
-        copy.wait_send()
-    for step in Z_STEPS:
-        far_copy(step, 0, 0).wait_send()
-
-    @pl.when(far_x != x)
+    for target, count, send in sent:
+        all_bytes(target, count, send).wait()
+
+    @pl.when(from_own)
     def _():
-        far_copy(0, 0, 0).wait_send()
+        all_bytes(zs.at[1, 0], 15, z_send.at[1, 0]).wait()
+
+    @pl.when(jnp.logical_not(from_own))
+    def _():
+        all_bytes(zs.at[1, 0], 16, z_send.at[1, 0]).wait()
 
 
 def body(pair_state, *weights):
@@ -389,10 +373,9 @@
             pltpu.VMEM((96, 128), bf16),
             pltpu.VMEM((2, 2, 16, 24, 128), bf16),
             pltpu.VMEM((2, 2, 16, 24, 128), bf16),
-            pltpu.VMEM((192, 128), f32),
             pltpu.VMEM((384, 128), f32),
-            pltpu.VMEM((2, 2, 8, 24, 128), bf16),
-            pltpu.VMEM((2, 2, 32, 24, 128), bf16),
+            pltpu.VMEM((2, 8, 48, 128), bf16),
+            pltpu.VMEM((2, 32, 48, 128), bf16),
             pltpu.VMEM((2, 8, 48, 128), bf16),
             pltpu.VMEM((2, 32, 48, 128), bf16),
             pltpu.VMEM((2, 8, 48, 128), bf16),
@@ -400,11 +383,11 @@
             pltpu.VMEM((2, 16, 24, 128), bf16),
             pltpu.VMEM((2, 16, 24, 128), bf16),
             dma((7,)),
-            dma((2, 2, 16)), dma((2, 2, 16)),
-            dma((2, 2, 32)), dma((2, 2, 32)),
-            dma((2, 8)), dma((2, 32)),
-            dma((2, 8)), dma((2, 32)),
-            dma((2, 16)), dma((2, 16)),
+            dma((2, 2)), dma((2, 2)),
+            dma((2,)), dma((2,)),
+            dma((2,)), dma((2,)),
+            dma((2,)), dma((2,)),
+            dma((2,)), dma((2,)),
         ],
         compiler_params=pltpu.CompilerParams(
             collective_id=0, has_side_effects=True, vmem_limit_bytes=60 * 2**20

time: 85 us -> 79.4 us (0.934)
  Pallas kernels: 82.2 us -> 76.7 us
    pallas_call x1, Pallas kernels: 82.2 us -> 76.7 us  [body(): pl.pallas_call(kernel, out_shape=jax.ShapeDtypeStruct((12, 24, 128), bf16...]
where the time goes in v4:
time: 79.4 us; the launch traced here: 78.3 us
  Pallas kernels  76.7 us (97%)
  local copies, waits for them, and re-layouts  1.52 us (2%)
    pallas_call x1, Pallas kernels, body(): pl.pallas_call(kernel, out_shape=jax.ShapeDtypeStruct((12, 24, 128), bf16...  76.7 us

profile of v4, /device:TPU:1, one launch (start us, length us, event | category | flops | bytes accessed | tf_op | source)
XLA Modules:
  0.0 78.3 jit_solution(12994928707496579425)
XLA Ops:
  0.0 76.7 %shard_map.73 = bf16[12,24,128]{2,1,0:T(8,128)(2,1)} custom-call(bf16[12,24,128]{2,1,0:T(8,128)(2,1)} %bitcast.3, bf16[128,640]{1,0:T(8,128)(2,1)} %w1_hbm.1, bf16[128,128]{1,0:T(8,128)(2,1)} %o1_hbm.1, bf16[128,640]{1,0:T(8,128)(2,1)} %w2_hbm.1, bf16[128,128]{1,0:T(8,128)(2,1)} %o2_hbm.1, bf16[128,1024]{1,0:T(8,128)(2,1)} %t1_hbm.1, bf16[512,128]{1,0:T(8,128)(2,1)} %t2_hbm.1), custom_call_target="tpu_custom_call" | custom-call | tf_op jit(solution)/shard_map/pallas_call | solution.py:363
  76.7 1.5 %copy.9 = bf16[24,12,128]{2,0,1:T(8,128)(2,1)} copy(bf16[24,12,128]{2,0,1:T(8,128)(2,1)} %bitcast.2) | data formatting | bytes 147456

commit v5 on v4

--- a/solution.py
+++ b/solution.py
@@ -11,13 +11,18 @@
 bf16 = jnp.bfloat16
 
 Z_STEPS = (8, 7, 9, 6, 10, 5, 11, 4, 12, 3, 13, 2, 14, 1, 15)
-RING = (2, 1, 3, 0)
-P_STEPS = tuple((0, dy, dc) for dy in RING for dc in (1, 0) if (dy, dc) != (0, 0))
-G_STEPS = tuple(
-    sorted(
-        ((dx, dy, dc) for dx in RING for dy in RING for dc in (1, 0) if (dx, dy, dc) != (0, 0, 0)),
-        key=lambda step: -(min(step[0], 4 - step[0]) + min(step[1], 4 - step[1])),
-    )
+
+
+def far_first(steps):
+    def hops(step):
+        return min(step[0], 4 - step[0]) + min(step[1], 4 - step[1]) + step[2]
+
+    return tuple(sorted(steps, key=lambda step: (-hops(step), -min(step[1], 4 - step[1]), step[0], step[1])))
+
+
+P_STEPS = far_first((0, dy, dc) for dy in range(4) for dc in range(2) if (dy, dc) != (0, 0))
+G_STEPS = far_first(
+    (dx, dy, dc) for dx in range(4) for dy in range(4) for dc in range(2) if (dx, dy, dc) != (0, 0, 0)
 )
 
 
@@ -91,6 +96,27 @@
             yield ih * 8 + il, swapped[il]
 
 
+def pack_rows(rows, roll):
+    spare = (lax.broadcasted_iota(jnp.int32, rows[0].shape, 1) & 15) >= 12
+    packed = list(rows[:40])
+    for third in range(3):
+        for a in range(8):
+            b = third * 8 + a
+            packed[b] = jnp.where(spare, roll(rows[40 + a], 12 - 4 * third), packed[b])
+    return packed
+
+
+def unpack_rows(packed, roll):
+    count = packed.shape[0]
+    packed = packed.astype(f32)
+    thirds = [
+        roll(packed[:, third * 8 : third * 8 + 8].reshape(count * 8, 128), 116 + 4 * third) for third in range(3)
+    ]
+    inside = lax.broadcasted_iota(jnp.int32, thirds[0].shape, 1) & 15
+    last = jnp.where(inside < 4, thirds[0], jnp.where(inside < 8, thirds[1], thirds[2]))
+    return jnp.concatenate([packed, last.reshape(count, 8, 128)], axis=1).astype(bf16)
+
+
 def assemble(parts):
     return jnp.concatenate(
         [
@@ -129,7 +155,7 @@
 def kernel(
     x_hbm, w1_hbm, o1_hbm, w2_hbm, o2_hbm, t1_hbm, t2_hbm, out_ref,
     x_ref, w1_ref, o1_ref, w2_ref, o2_ref, t1_ref, t2_ref,
-    block, columns, rows, zs, zr, wide, rs, rr, ls, ll, c1s, c1r, c2s, c2r,
+    block, columns, rows, zs, zr, wide, narrow, rs, rr, ls, ll, c1s, c1r, c2s, c2r,
     load_sem, z_send, z_recv, r_send, r_recv, l_send, l_recv, c1_send, c1_recv, c2_send, c2_recv,
 ):
     row, col = lax.axis_index("row"), lax.axis_index("col")
@@ -250,11 +276,15 @@
         gate = jax.nn.sigmoid(nn(normed, w_ref[:, 512:640]))
 
         arrive(*right_z)
-        for zh_ in range(2):
-            for i, values in regroup([zr[n, 1, zh_ * 8 + zl_].astype(f32) for zl_ in range(8)], roll_lanes):
-                wide[pl.ds(zh_ * 24 + i, 8, stride=48), :] = values
+        values = [
+            value
+            for zh_ in range(2)
+            for _, value in regroup([zr[n, 1, zh_ * 8 + zl_].astype(f32) for zl_ in range(8)], roll_lanes)
+        ]
+        for i, value in enumerate(pack_rows(values, roll_lanes)):
+            narrow[pl.ds(i, 8, stride=40), :] = value
         for c in range(8):
-            rs[n, c] = wide[c * 48 : c * 48 + 48, :].astype(bf16)
+            rs[n, c] = narrow[c * 40 : c * 40 + 40, :].astype(bf16)
         right_g = (
             g_peer, G_STEPS, lambda other: rs.at[n, lax.rem(other, 8)], rr.at[n], g,
             r_send.at[n], r_recv.at[n],
@@ -290,7 +320,8 @@
         exchange(*left_g)
         ll[n, g] = ls[n, p]
         arrive(*right_g)
-        rights = assemble(lambda x_, p_: rr[n, x_ * 8 + p_])
+        unpacked = unpack_rows(rr[n], roll_lanes)
+        rights = assemble(lambda x_, p_: unpacked[x_ * 8 + p_])
         arrive(*left_g)
         if n == 0:
             lefts = jnp.concatenate(
@@ -374,8 +405,9 @@
             pltpu.VMEM((2, 2, 16, 24, 128), bf16),
             pltpu.VMEM((2, 2, 16, 24, 128), bf16),
             pltpu.VMEM((384, 128), f32),
-            pltpu.VMEM((2, 8, 48, 128), bf16),
-            pltpu.VMEM((2, 32, 48, 128), bf16),
+            pltpu.VMEM((320, 128), f32),
+            pltpu.VMEM((2, 8, 40, 128), bf16),
+            pltpu.VMEM((2, 32, 40, 128), bf16),
             pltpu.VMEM((2, 8, 48, 128), bf16),
             pltpu.VMEM((2, 32, 48, 128), bf16),
             pltpu.VMEM((2, 8, 48, 128), bf16),

time: 79.4 us -> 79.3 us (level)
  no operation moved by 1% of the time
where the time goes in v5:
time: 79.3 us; the launch traced here: 78.3 us
  Pallas kernels  76.8 us (97%)
  local copies, waits for them, and re-layouts  1.52 us (2%)
    pallas_call x1, Pallas kernels, body(): pl.pallas_call(kernel, out_shape=jax.ShapeDtypeStruct((12, 24, 128), bf16...  76.8 us

profile of v5, /device:TPU:1, one launch (start us, length us, event | category | flops | bytes accessed | tf_op | source)
XLA Modules:
  0.0 78.3 jit_solution(7000053137821963282)
XLA Ops:
  0.0 76.8 %shard_map.73 = bf16[12,24,128]{2,1,0:T(8,128)(2,1)} custom-call(bf16[12,24,128]{2,1,0:T(8,128)(2,1)} %bitcast.3, bf16[128,640]{1,0:T(8,128)(2,1)} %w1_hbm.1, bf16[128,128]{1,0:T(8,128)(2,1)} %o1_hbm.1, bf16[128,640]{1,0:T(8,128)(2,1)} %w2_hbm.1, bf16[128,128]{1,0:T(8,128)(2,1)} %o2_hbm.1, bf16[128,1024]{1,0:T(8,128)(2,1)} %t1_hbm.1, bf16[512,128]{1,0:T(8,128)(2,1)} %t2_hbm.1), custom_call_target="tpu_custom_call" | custom-call | tf_op jit(solution)/shard_map/pallas_call | solution.py:394
  76.8 1.5 %copy.9 = bf16[24,12,128]{2,0,1:T(8,128)(2,1)} copy(bf16[24,12,128]{2,0,1:T(8,128)(2,1)} %bitcast.2) | data formatting | bytes 147456

commit v6 on v5

--- a/solution.py
+++ b/solution.py
@@ -85,8 +85,26 @@
     return jax.nn.sigmoid(projected[0:128]) * projected[128:256]
 
 
-def z_parcel(values, z):
-    return jnp.concatenate([values[z * 8 : z * 8 + 8, ih * 128 : ih * 128 + 128] for ih in range(3)], axis=0)
+def z_parcel(values, z, groups=3):
+    return jnp.concatenate([values[z * 8 : z * 8 + 8, ih * 128 : ih * 128 + 128] for ih in range(groups)], axis=0)
+
+
+def lend_lanes(right, left, roll):
+    spare = (lax.broadcasted_iota(jnp.int32, (128, 128), 1) & 15) >= 12
+    return jnp.concatenate(
+        [
+            jnp.where(spare, roll(left[:, 256:384], 12 - 4 * ih), right[:, ih * 128 : ih * 128 + 128])
+            for ih in range(3)
+        ],
+        axis=1,
+    )
+
+
+def lent_rows(right, roll):
+    thirds = [roll(right[ih * 8 : ih * 8 + 8], 116 + 4 * ih) for ih in range(3)]
+    inside = lax.broadcasted_iota(jnp.int32, (8, 128), 1) & 15
+    last = jnp.where(inside < 12, thirds[2], 0.0)
+    return jnp.where(inside < 4, thirds[0], jnp.where(inside < 8, thirds[1], last))
 
 
 def regroup(parts, roll):
@@ -155,7 +173,7 @@
 def kernel(
     x_hbm, w1_hbm, o1_hbm, w2_hbm, o2_hbm, t1_hbm, t2_hbm, out_ref,
     x_ref, w1_ref, o1_ref, w2_ref, o2_ref, t1_ref, t2_ref,
-    block, columns, rows, zs, zr, wide, narrow, rs, rr, ls, ll, c1s, c1r, c2s, c2r,
+    block, columns, rows, zs, zr, short_s, short_r, wide, narrow, rs, rr, ls, ll, c1s, c1r, c2s, c2r,
     load_sem, z_send, z_recv, r_send, r_recv, l_send, l_recv, c1_send, c1_recv, c2_send, c2_recv,
 ):
     row, col = lax.axis_index("row"), lax.axis_index("col")
@@ -238,30 +256,39 @@
         ordered = order_rows(normed)
         (first_loads[1] if n == 0 else later[1]).wait()
 
-        def fill_z(s):
-            values = edge(ordered, w_ref[:, s * 256 : s * 256 + 256].T)
-            for other in range(16):
-                zs[n, s, other] = z_parcel(values, other).astype(bf16)
-            return (
-                z_peer, Z_STEPS, lambda other: zs.at[n, s, other], zr.at[n, s], z,
-                z_send.at[n, s], z_recv.at[n, s],
-            )
-
-        right_z = fill_z(1)
+        def edges(s):
+            return edge(ordered, w_ref[:, s * 256 : s * 256 + 256].T)
+
+        right = edges(1)
+        if n == 0:
+            left = edges(0)
+            right = lend_lanes(right, left, roll_lanes)
+        for other in range(16):
+            zs[n, 1, other] = z_parcel(right, other).astype(bf16)
+        right_z = (
+            z_peer, Z_STEPS, lambda other: zs.at[n, 1, other], zr.at[n, 1], z, z_send.at[n, 1], z_recv.at[n, 1]
+        )
         if n == 0:
             pl.semaphore_wait(barrier, greeted)
         exchange(*right_z)
         zr[n, 1, z] = zs[n, 1, z]
-        left_z = fill_z(0)
         slot = x * 4 + zh * 2 + lax.rem(zl, 2)
         if n == 0:
+            for other in range(16):
+                short_s[other] = z_parcel(left, other, 2).astype(bf16)
+            left_z = (
+                z_peer, Z_STEPS, lambda other: short_s.at[other], short_r, z, z_send.at[n, 0], z_recv.at[n, 0]
+            )
             exchange(*left_z)
-            zr[n, 0, z] = zs[n, 0, z]
+            short_r[z] = short_s[z]
             for i, (source, target) in enumerate(
                 ((o1_hbm, o1_ref), (w2_hbm, w2_ref), (o2_hbm, o2_ref), (t1_hbm, t1_ref), (t2_hbm, t2_ref))
             ):
                 later.append(load(2 + i, source, target))
         else:
+            left = edges(0)
+            for other in range(16):
+                zs[n, 0, other] = z_parcel(left, other).astype(bf16)
             for step in Z_STEPS:
                 far_copy(step)
 
@@ -294,7 +321,19 @@
 
         if n == 0:
             arrive(*left_z)
-            parts = [[zr[n, 0, zh_ * 8 + zl_].astype(f32) for zl_ in range(8)] for zh_ in range(2)]
+            parts = [
+                [
+                    jnp.concatenate(
+                        [
+                            short_r[zh_ * 8 + zl_].astype(f32),
+                            lent_rows(zr[n, 1, zh_ * 8 + zl_].astype(f32), roll_lanes),
+                        ],
+                        axis=0,
+                    )
+                    for zl_ in range(8)
+                ]
+                for zh_ in range(2)
+            ]
         else:
             @pl.when(from_own)
             def _():
@@ -404,6 +443,8 @@
             pltpu.VMEM((96, 128), bf16),
             pltpu.VMEM((2, 2, 16, 24, 128), bf16),
             pltpu.VMEM((2, 2, 16, 24, 128), bf16),
+            pltpu.VMEM((16, 16, 128), bf16),
+            pltpu.VMEM((16, 16, 128), bf16),
             pltpu.VMEM((384, 128), f32),
             pltpu.VMEM((320, 128), f32),
             pltpu.VMEM((2, 8, 40, 128), bf16),

time: 79.3 us -> 78.3 us (0.987)
  Pallas kernels: 76.8 us -> 76 us
    pallas_call x1, Pallas kernels: 76.8 us -> 76 us  [body(): pl.pallas_call(kernel, out_shape=jax.ShapeDtypeStruct((12, 24, 128), bf16...]
where the time goes in v6:
time: 78.3 us; the launch traced here: 77.5 us
  Pallas kernels  76 us (97%)
  local copies, waits for them, and re-layouts  1.52 us (2%)
    pallas_call x1, Pallas kernels, body(): pl.pallas_call(kernel, out_shape=jax.ShapeDtypeStruct((12, 24, 128), bf16...  76 us

profile of v6, /device:TPU:1, one launch (start us, length us, event | category | flops | bytes accessed | tf_op | source)
XLA Modules:
  0.0 77.5 jit_solution(18301238184604706827)
XLA Ops:
  0.0 76.0 %shard_map.73 = bf16[12,24,128]{2,1,0:T(8,128)(2,1)} custom-call(bf16[12,24,128]{2,1,0:T(8,128)(2,1)} %bitcast.3, bf16[128,640]{1,0:T(8,128)(2,1)} %w1_hbm.1, bf16[128,128]{1,0:T(8,128)(2,1)} %o1_hbm.1, bf16[128,640]{1,0:T(8,128)(2,1)} %w2_hbm.1, bf16[128,128]{1,0:T(8,128)(2,1)} %o2_hbm.1, bf16[128,1024]{1,0:T(8,128)(2,1)} %t1_hbm.1, bf16[512,128]{1,0:T(8,128)(2,1)} %t2_hbm.1), custom_call_target="tpu_custom_call" | custom-call | tf_op jit(solution)/shard_map/pallas_call | solution.py:433
  76.0 1.5 %copy.9 = bf16[24,12,128]{2,0,1:T(8,128)(2,1)} copy(bf16[24,12,128]{2,0,1:T(8,128)(2,1)} %bitcast.2) | data formatting | bytes 147456

commit v7 on v6

--- a/solution.py
+++ b/solution.py
@@ -406,16 +406,18 @@
     state = block[...].astype(bf16)
     state = triangle(0, state, w1_ref, o1_ref)
     state = triangle(1, state, w2_ref, o2_ref)
-    normed = layer_norm(state.astype(f32)).astype(bf16)
+    block[...] = state.astype(f32)
+    state = jnp.concatenate(
+        [block[pl.ds(ih * 16 + k, 8, stride=48), :] for k in range(12) for ih in range(3)], axis=0
+    )
+    normed = layer_norm(state).astype(bf16)
     later[3].wait()
     later[4].wait()
     hidden = nn(normed, t1_ref[...])
     mixed = (jax.nn.silu(hidden[:, :512]) * hidden[:, 512:]).astype(bf16)
-    block[...] = state.astype(f32) + nn(mixed, t2_ref[...])
+    result = (state + nn(mixed, t2_ref[...])).astype(bf16)
     for k in range(12):
-        out_ref[k] = jnp.concatenate(
-            [block[pl.ds(ih * 16 + k, 8, stride=48), :] for ih in range(3)], axis=0
-        ).astype(bf16)
+        out_ref[k] = result[k * 24 : k * 24 + 24]
     for target, count, send in sent:
         all_bytes(target, count, send).wait()
 

time: 78.3 us -> 78.2 us (level)
  no operation moved by 1% of the time
where the time goes in v7:
time: 78.2 us; the launch traced here: 77.4 us
  Pallas kernels  75.9 us (97%)
  local copies, waits for them, and re-layouts  1.52 us (2%)
    pallas_call x1, Pallas kernels, body(): pl.pallas_call(kernel, out_shape=jax.ShapeDtypeStruct((12, 24, 128), bf16...  75.9 us

profile of v7, /device:TPU:1, one launch (start us, length us, event | category | flops | bytes accessed | tf_op | source)
XLA Modules:
  0.0 77.4 jit_solution(11232709665084105172)
XLA Ops:
  0.0 75.9 %shard_map.73 = bf16[12,24,128]{2,1,0:T(8,128)(2,1)} custom-call(bf16[12,24,128]{2,1,0:T(8,128)(2,1)} %bitcast.3, bf16[128,640]{1,0:T(8,128)(2,1)} %w1_hbm.1, bf16[128,128]{1,0:T(8,128)(2,1)} %o1_hbm.1, bf16[128,640]{1,0:T(8,128)(2,1)} %w2_hbm.1, bf16[128,128]{1,0:T(8,128)(2,1)} %o2_hbm.1, bf16[128,1024]{1,0:T(8,128)(2,1)} %t1_hbm.1, bf16[512,128]{1,0:T(8,128)(2,1)} %t2_hbm.1), custom_call_target="tpu_custom_call" | custom-call | tf_op jit(solution)/shard_map/pallas_call | solution.py:435
  75.9 1.5 %copy.9 = bf16[24,12,128]{2,0,1:T(8,128)(2,1)} copy(bf16[24,12,128]{2,0,1:T(8,128)(2,1)} %bitcast.2) | data formatting | bytes 147456

commit v8 on v6

--- a/solution.py
+++ b/solution.py
@@ -124,7 +124,7 @@
     return packed
 
 
-def unpack_rows(packed, roll):
+def unpack_rows(packed, roll, clean=False):
     count = packed.shape[0]
     packed = packed.astype(f32)
     thirds = [
@@ -132,7 +132,10 @@
     ]
     inside = lax.broadcasted_iota(jnp.int32, thirds[0].shape, 1) & 15
     last = jnp.where(inside < 4, thirds[0], jnp.where(inside < 8, thirds[1], thirds[2]))
-    return jnp.concatenate([packed, last.reshape(count, 8, 128)], axis=1).astype(bf16)
+    whole = jnp.concatenate([packed, last.reshape(count, 8, 128)], axis=1)
+    if clean:
+        whole = jnp.where((lax.broadcasted_iota(jnp.int32, whole.shape, 2) & 15) < 12, whole, 0.0)
+    return whole.astype(bf16)
 
 
 def assemble(parts):
@@ -347,11 +350,11 @@
                 [zr[n, 0, x_ * 4 + zh_ * 2 + zlo].astype(f32) for x_ in range(4) for zlo in range(2)]
                 for zh_ in range(2)
             ]
-        for zh_ in range(2):
-            for i, values in regroup(parts[zh_], roll_lanes):
-                wide[pl.ds(zh_ * 24 + i, 8, stride=48), :] = values
+        values = [value for zh_ in range(2) for _, value in regroup(parts[zh_], roll_lanes)]
+        for i, value in enumerate(pack_rows(values, roll_lanes)):
+            wide[pl.ds(i, 8, stride=40), :] = value
         for c in range(8):
-            ls[n, c] = wide[c * 48 : c * 48 + 48, :].astype(bf16)
+            ls[n, c] = wide[c * 40 : c * 40 + 40, :].astype(bf16)
         left_g = (
             g_peer, P_STEPS, lambda other: ls.at[n, lax.rem(other, 8)], ll.at[n], g,
             l_send.at[n], l_recv.at[n],
@@ -362,17 +365,18 @@
         unpacked = unpack_rows(rr[n], roll_lanes)
         rights = assemble(lambda x_, p_: unpacked[x_ * 8 + p_])
         arrive(*left_g)
+        own = unpack_rows(ll[n, pl.ds(x * 8, 8)], roll_lanes, clean=n == 0)
         if n == 0:
             lefts = jnp.concatenate(
                 [
-                    jnp.concatenate([ll[n, x * 8 + y_ * 2 + core_] for y_ in range(4)], axis=1)
+                    jnp.concatenate([own[y_ * 2 + core_] for y_ in range(4)], axis=1)
                     for core_ in range(2)
                 ],
                 axis=0,
             )
             total = product_out(lefts, rights, columns[...])
         else:
-            total = product_in(lambda p_: ll[n, x * 8 + p_], rights, rows[...], roll_lanes)
+            total = product_in(lambda p_: own[p_], rights, rows[...], roll_lanes)
 
         for other in range(8):
             there, far = other % 2, other // 2
@@ -445,12 +449,12 @@
             pltpu.VMEM((2, 2, 16, 24, 128), bf16),
             pltpu.VMEM((16, 16, 128), bf16),
             pltpu.VMEM((16, 16, 128), bf16),
-            pltpu.VMEM((384, 128), f32),
+            pltpu.VMEM((320, 128), f32),
             pltpu.VMEM((320, 128), f32),
             pltpu.VMEM((2, 8, 40, 128), bf16),
             pltpu.VMEM((2, 32, 40, 128), bf16),
-            pltpu.VMEM((2, 8, 48, 128), bf16),
-            pltpu.VMEM((2, 32, 48, 128), bf16),
+            pltpu.VMEM((2, 8, 40, 128), bf16),
+            pltpu.VMEM((2, 32, 40, 128), bf16),
             pltpu.VMEM((2, 8, 48, 128), bf16),
             pltpu.VMEM((2, 32, 48, 128), bf16),
             pltpu.VMEM((2, 16, 24, 128), bf16),

time: 78.3 us -> 78.3 us (level)
  no operation moved by 1% of the time
where the time goes in v8:
time: 78.3 us; the launch traced here: 77.8 us
  Pallas kernels  76.3 us (97%)
  local copies, waits for them, and re-layouts  1.52 us (2%)
    pallas_call x1, Pallas kernels, body(): pl.pallas_call(kernel, out_shape=jax.ShapeDtypeStruct((12, 24, 128), bf16...  76.3 us

profile of v8, /device:TPU:1, one launch (start us, length us, event | category | flops | bytes accessed | tf_op | source)
XLA Modules:
  0.0 77.8 jit_solution(5554522347416402379)
XLA Ops:
  0.0 76.3 %shard_map.73 = bf16[12,24,128]{2,1,0:T(8,128)(2,1)} custom-call(bf16[12,24,128]{2,1,0:T(8,128)(2,1)} %bitcast.3, bf16[128,640]{1,0:T(8,128)(2,1)} %w1_hbm.1, bf16[128,128]{1,0:T(8,128)(2,1)} %o1_hbm.1, bf16[128,640]{1,0:T(8,128)(2,1)} %w2_hbm.1, bf16[128,128]{1,0:T(8,128)(2,1)} %o2_hbm.1, bf16[128,1024]{1,0:T(8,128)(2,1)} %t1_hbm.1, bf16[512,128]{1,0:T(8,128)(2,1)} %t2_hbm.1), custom_call_target="tpu_custom_call" | custom-call | tf_op jit(solution)/shard_map/pallas_call | solution.py:437
  76.3 1.5 %copy.9 = bf16[24,12,128]{2,0,1:T(8,128)(2,1)} copy(bf16[24,12,128]{2,0,1:T(8,128)(2,1)} %bitcast.2) | data formatting | bytes 147456

commit v9 on v6

--- a/solution.py
+++ b/solution.py
@@ -225,14 +225,15 @@
 
     sent = []
 
-    def exchange(peer, steps, source, target, me, send, recv):
-        for step in steps:
+    def exchange(peer, steps, source, target, me, send, recv, part=None):
+        for step in steps if part is None else part:
             other, place = peer(step)
             pltpu.make_async_remote_copy(
                 src_ref=source(other), dst_ref=target.at[me], send_sem=send, recv_sem=recv,
                 device_id=place, device_id_type=MESH,
             ).start()
-        sent.append((target, len(steps), send))
+        if part is None or part[-1] == steps[-1]:
+            sent.append((target, len(steps), send))
 
     def all_bytes(target, count, sem):
         blocks = target.at[pl.ds(0, count)]
@@ -270,7 +271,7 @@
         )
         if n == 0:
             pl.semaphore_wait(barrier, greeted)
-        exchange(*right_z)
+        exchange(*right_z, part=Z_STEPS[:9] if n == 0 else None)
         zr[n, 1, z] = zs[n, 1, z]
         slot = x * 4 + zh * 2 + lax.rem(zl, 2)
         if n == 0:
@@ -279,7 +280,9 @@
             left_z = (
                 z_peer, Z_STEPS, lambda other: short_s.at[other], short_r, z, z_send.at[n, 0], z_recv.at[n, 0]
             )
-            exchange(*left_z)
+            exchange(*left_z, part=Z_STEPS[:9])
+            exchange(*right_z, part=Z_STEPS[9:])
+            exchange(*left_z, part=Z_STEPS[9:])
             short_r[z] = short_s[z]
             for i, (source, target) in enumerate(
                 ((o1_hbm, o1_ref), (w2_hbm, w2_ref), (o2_hbm, o2_ref), (t1_hbm, t1_ref), (t2_hbm, t2_ref))

time: 78.3 us -> 78.6 us (level)
  no operation moved by 1% of the time
where the time goes in v9:
time: 78.6 us; the launch traced here: 77.7 us
  Pallas kernels  76.1 us (97%)
  local copies, waits for them, and re-layouts  1.52 us (2%)
    pallas_call x1, Pallas kernels, body(): pl.pallas_call(kernel, out_shape=jax.ShapeDtypeStruct((12, 24, 128), bf16...  76.1 us

profile of v9, /device:TPU:1, one launch (start us, length us, event | category | flops | bytes accessed | tf_op | source)
XLA Modules:
  0.0 77.7 jit_solution(8149149406340728789)
XLA Ops:
  0.0 76.1 %shard_map.73 = bf16[12,24,128]{2,1,0:T(8,128)(2,1)} custom-call(bf16[12,24,128]{2,1,0:T(8,128)(2,1)} %bitcast.3, bf16[128,640]{1,0:T(8,128)(2,1)} %w1_hbm.1, bf16[128,128]{1,0:T(8,128)(2,1)} %o1_hbm.1, bf16[128,640]{1,0:T(8,128)(2,1)} %w2_hbm.1, bf16[128,128]{1,0:T(8,128)(2,1)} %o2_hbm.1, bf16[128,1024]{1,0:T(8,128)(2,1)} %t1_hbm.1, bf16[512,128]{1,0:T(8,128)(2,1)} %t2_hbm.1), custom_call_target="tpu_custom_call" | custom-call | tf_op jit(solution)/shard_map/pallas_call | solution.py:436
  76.2 1.5 %copy.9 = bf16[24,12,128]{2,0,1:T(8,128)(2,1)} copy(bf16[24,12,128]{2,0,1:T(8,128)(2,1)} %bitcast.2) | data formatting | bytes 147456
